TPU v7x, 32 devices: a whole 2x2x4 slice. The times are simulated.
32 devices in a mesh: rep: 8 (over z, x), shard: 4 (over y, core).
Axes of the slice: x: 2, y: 2, z: 4, core: 2. Of those that a mesh axis runs over, the one named last changes fastest.
Arguments:
- tokens: bfloat16 [32768, 1024], P(('rep', 'shard')), may hold values from -6 to 6
- segment_ids: int32 [32, 1024], P(('rep', 'shard')), may hold values from 0 to 3, never falling along the last dimension, each value on 1 to 800 neighbouring positions
- norm_gain_one: bfloat16 [1024], P('shard'), may hold values from 0.5 to 1.5
- w_query: bfloat16 [1024, 256], P('shard'), may hold values from -0.1875 to 0.1875
- w_key: bfloat16 [1024, 256], P('shard'), may hold values from -0.1875 to 0.1875
- w_value: bfloat16 [1024, 1024], P('shard'), may hold values from -0.1875 to 0.1875
- w_convgate: bfloat16 [1024, 1024], P('shard'), may hold values from -0.1875 to 0.1875
- w_output: bfloat16 [1024, 1024], P('shard'), may hold values from -0.375 to 0.375
- conv_filter: bfloat16 [3, 1024], P(None, 'shard'), may hold values from -2.390625 to 2.390625
- norm_gain_two: bfloat16 [1024], P('shard'), may hold values from 0.5 to 1.5
- w_gate: bfloat16 [1024, 4096], P('shard'), may hold values from -0.1875 to 0.1875
- w_up: bfloat16 [1024, 4096], P('shard'), may hold values from -0.1875 to 0.1875
- w_down: bfloat16 [4096, 1024], P('shard'), may hold values from -0.1875 to 0.1875
- cotangent: bfloat16 [32768, 1024], P(('rep', 'shard')), may hold values from -6 to 6
Outputs:
- out: bfloat16 [32768, 1024], P(('rep', 'shard'))
- grad_tokens: float32 [32768, 1024], P(('rep', 'shard'))
- grad_gain_one: float32 [1024], P('shard')
- grad_query: float32 [1024, 256], P('shard')
- grad_key: float32 [1024, 256], P('shard')
- grad_value: float32 [1024, 1024], P('shard')
- grad_convgate: float32 [1024, 1024], P('shard')
- grad_output: float32 [1024, 1024], P('shard')
- grad_filter: float32 [3, 1024], P(None, 'shard')
- grad_gain_two: float32 [1024], P('shard')
- grad_gate: float32 [1024, 4096], P('shard')
- grad_up: float32 [1024, 4096], P('shard')
- grad_down: float32 [4096, 1024], P('shard')
Inputs may be any that keep to these rules, and one draw needn't show every extreme that they name: `segment_ids`: along each sequence the document numbers never fall; a document holds at most 800 tokens.
All inputs are finite; a program needn't handle non-finite values.
Results may differ from a plain program's by a relative error of at most 0.02.
Values may be sent and summed in bfloat16 or wider, within the bound.
No kernel may reach another device: no remote copies, remote signals or barrier semaphores. Data moves between devices by JAX's collectives and lax.ppermute only.
A program may use at most 256 MiB of HBM per device.

v0:
```python
import functools

import jax
import jax.numpy as jnp
import numpy as np
from jax import lax
from jax.experimental import pallas as pl
from jax.experimental.pallas import tpu as pltpu
from jax.sharding import Mesh
from jax.sharding import PartitionSpec as P

HEADS = 16
FEAT = 16
KW = 3
EPS = 1e-06
TILE = 256
SHARD_ROWS = 256
LANES = 128
TICK = 1e5
X_AT, MIXER_AT, FEED_AT, DOWN_AT, PACK_AT, COLS_AT, GRAD_AT, OWNER_AT, ACT_AT, QUARTER_AT = 0, 2, 12, 16, 20, 28, 36, 40, 44, 48

low = jnp.bfloat16
wide = jnp.float32


def dot(a, b):
    return jnp.dot(a, b, preferred_element_type=wide)


def dot_nt(a, b):
    return lax.dot_general(a, b, (((1,), (1,)), ((), ())), preferred_element_type=wide)


def dot_tn(a, b):
    return lax.dot_general(a, b, (((0,), (0,)), ((), ())), preferred_element_type=wide)


class Order:
    last = None
    scale = 1.0


def launch(kernel, deps=(), onto=(), *, scalars=0, grid, in_specs, out_specs, out_shape, scratch_shapes=(), **rest):
    taken = scalars + len(in_specs)
    deps = list(onto) + [d for d in deps if d is not None] + ([] if Order.last is None or any(Order.last is a for a in onto) else [Order.last])

    def body(*refs):
        kernel(*refs[:taken], *refs[taken + len(deps) :])

    spec = pltpu.PrefetchScalarGridSpec(
        num_scalar_prefetch=scalars,
        grid=grid,
        in_specs=list(in_specs) + [pl.BlockSpec(memory_space=pl.ANY)] * len(deps),
        out_specs=out_specs,
        scratch_shapes=list(scratch_shapes),
    )
    aliases = {taken + n: n for n in range(len(onto))}
    run = pl.pallas_call(body, grid_spec=spec, out_shape=out_shape, input_output_aliases=aliases, **rest)

    def call(*operands):
        result = run(*operands, *deps)
        Order.last = result[0] if isinstance(result, (list, tuple)) else result
        return result

    return call


def params(mib, least=60):
    return pltpu.CompilerParams(vmem_limit_bytes=max(mib, least) << 20)


def cost(gigaflops, mebibytes):
    return pl.CostEstimate(
        flops=int(gigaflops * Order.scale * 1e9), bytes_accessed=int(mebibytes * Order.scale * (1 << 20)), transcendentals=0
    )


def fixed(shape):
    return pl.BlockSpec(shape, lambda *_: (0,) * len(shape), pipeline_mode=pl.Buffered(1))


def rows(height, width):
    return pl.BlockSpec((height, width), lambda i, *_: (i, 0))


def place(offs_ref, base, pieces, full_ref):
    for n, piece in enumerate(pieces):
        at = pl.multiple_of(offs_ref[base + n], 64)
        full_ref[pl.ds(at, piece.shape[0]), :] = piece[...]


def project_kernel(offs_ref, x_ref, *refs):
    pieces, (hidden_ref, q_ref, k_ref, v_ref, gate_ref, vec_ref, out_ref, full_ref, sem) = refs[:10], refs[10:]
    copy = pltpu.make_async_copy(full_ref, out_ref, sem)
    heads = HEADS * FEAT
    width = x_ref.shape[1]

    @pl.when(pl.program_id(0) == 0)
    def _():
        place(offs_ref, MIXER_AT, pieces, full_ref)
        copy.start()
        small = full_ref[:, 2 * heads + 3 * width :].astype(wide)
        vec_ref[...] = small.T[:8, :]

    x = x_ref[...].astype(wide)
    inverse = lax.rsqrt(jnp.mean(x * x, axis=-1, keepdims=True) + EPS)
    hidden = (x * inverse * vec_ref[0:1, :]).astype(low)
    hidden_ref[...] = hidden
    at = width
    q_ref[...] = (dot(hidden, full_ref[:, at : at + heads]) * FEAT ** (-0.5)).astype(low)
    k_ref[...] = dot(hidden, full_ref[:, at + heads : at + 2 * heads]).astype(low)
    at = at + 2 * heads
    v_ref[...] = dot(hidden, full_ref[:, at : at + width]).astype(low)
    gate_ref[...] = dot(hidden, full_ref[:, at + width : at + 2 * width]).astype(low)

    @pl.when(pl.program_id(0) == pl.num_programs(0) - 1)
    def _():
        copy.wait()


def project(offs, x, pieces, deps=()):
    length, width = x.shape
    heads = HEADS * FEAT
    columns = pieces[0].shape[1]
    shapes = [
        jax.ShapeDtypeStruct((length, width), low),
        jax.ShapeDtypeStruct((length, heads), low),
        jax.ShapeDtypeStruct((length, heads), low),
        jax.ShapeDtypeStruct((length, width), low),
        jax.ShapeDtypeStruct((length, width), low),
        jax.ShapeDtypeStruct((8, width), wide),
        jax.ShapeDtypeStruct((width, columns), low),
    ]
    return launch(
        project_kernel,
        deps,
        scalars=1,
        grid=(length // TILE,),
        in_specs=[rows(TILE, width)] + [fixed(p.shape) for p in pieces],
        out_specs=[
            rows(TILE, width),
            rows(TILE, heads),
            rows(TILE, heads),
            rows(TILE, width),
            rows(TILE, width),
            fixed((8, width)),
            pl.BlockSpec(memory_space=pl.ANY),
        ],
        scratch_shapes=[pltpu.VMEM((width, columns), low), pltpu.SemaphoreType.DMA],
        out_shape=shapes,
        compiler_params=params(40),
        cost_estimate=cost(7, 22),
        name="project",
    )(offs, x, *pieces)


def shift_rows(v, seg, by, up):
    zeros = jnp.zeros((by, v.shape[1]), v.dtype)
    none = jnp.full((by, 1), -1, seg.dtype)
    if up:
        moved, moved_seg = jnp.concatenate([v[by:], zeros], 0), jnp.concatenate([seg[by:], none], 0)
    else:
        moved = jnp.concatenate([zeros, v[:-by]], 0)
        moved_seg = jnp.concatenate([none, seg[:-by]], 0)
    return jnp.where(moved_seg == seg, moved, 0.0)


def lane_pick(width, start, stop):
    i = lax.broadcasted_iota(jnp.int32, (1, width), 1)
    return (i >= start) & (i < stop)


def attend_kernel(
    first, q_ref, k_ref, v_ref, gate_ref, vec_ref, segr_ref, segc_ref, mixed_ref, att_ref, recip_ref, mask_ref
):
    length = q_ref.shape[0]
    pair = pl.program_id(0) + first
    zero = jnp.zeros((), low)

    @pl.when(pair == first)
    def _():
        for tb in range(0, length, TILE):
            t = lax.broadcasted_iota(jnp.int32, (TILE, length), 0) + tb
            s = lax.broadcasted_iota(jnp.int32, (TILE, length), 1)
            seen = (s <= t) & (segc_ref[tb : tb + TILE, :] == segr_ref[...])
            mask_ref[tb : tb + TILE, :] = jnp.where(seen, 1.0, 0.0).astype(low)

    v = v_ref[...]
    keys, sides = [], []
    for i in range(2):
        head = 2 * pair + i
        keys.append(jnp.where(lane_pick(HEADS * FEAT, head * FEAT, (head + 1) * FEAT), k_ref[...], zero))
        lanes = lane_pick(128, 64 * i, 64 * i + 64)
        ones = jnp.broadcast_to(jnp.where(lanes, 1.0, 0.0).astype(low), (length, 128))
        sides.append(jnp.concatenate([jnp.where(lanes, v, zero), ones], 1))
    for tb in range(0, length, TILE):
        n = tb + TILE
        total = None
        for i in range(2):
            one_plus = dot_nt(q_ref[tb:n, :], keys[i][:n]) + 1.0
            kernel = (one_plus * one_plus + 1.0).astype(low) * mask_ref[tb:n, :n]
            part = dot(kernel, sides[i][:n])
            total = part if total is None else total + part
        recip = 1.0 / total[:, 128:]
        att_ref[tb:n, :] = (total[:, :128] * recip).astype(low)
        recip_ref[tb:n, :] = (2.0 * recip).astype(low)
    v_wide = v.astype(wide)
    seg = segc_ref[...]
    conv = vec_ref[2:3, :] * v_wide
    for j in range(1, KW):
        conv = conv + vec_ref[2 + j : 3 + j, :] * shift_rows(v_wide, seg, j, False)
    mixed_ref[...] = (att_ref[...].astype(wide) + gate_ref[...].astype(wide) * conv).astype(low)


def whole(a):
    return pl.BlockSpec(a.shape, lambda p: (0, 0))


def attend(q, k, v, gate, vec, seg, first, count, onto=(), deps=()):
    length, width = v.shape
    column = pl.BlockSpec((length, 128), lambda p: (0, p + first))
    seg_row, seg_col = seg.reshape(1, length), seg.reshape(length, 1)
    return launch(
        functools.partial(attend_kernel, first),
        deps,
        onto,
        grid=(count,),
        in_specs=[
            whole(q), whole(k), column, column, pl.BlockSpec((8, 128), lambda p: (0, p + first)), whole(seg_row), whole(seg_col)
        ],
        out_specs=[column] * 3,
        out_shape=[jax.ShapeDtypeStruct((length, width), low)] * 3,
        scratch_shapes=[pltpu.VMEM((length, length), low)],
        compiler_params=params(40),
        cost_estimate=cost(18 * count * 128 / width, 14),
        name="attention_forward",
    )(q, k, v, gate, vec, seg_row, seg_col)


def attend_back_kernel(
    first, q_ref, k_ref, v_ref, gm_ref, att_ref, recip_ref, gconv_ref, segr_ref, segc_ref,
    gqk_ref, gv_ref, mask_ref, gq_acc, gk_acc,
):
    length, heads = q_ref.shape
    pair = pl.program_id(0) + first
    zero = jnp.zeros((), low)

    @pl.when(pair == first)
    def _():
        for sb in range(0, length, TILE):
            s = lax.broadcasted_iota(jnp.int32, (TILE, length), 0) + sb
            t = lax.broadcasted_iota(jnp.int32, (TILE, length), 1)
            seen = (s <= t) & (segc_ref[sb : sb + TILE, :] == segr_ref[...])
            mask_ref[sb : sb + TILE, :] = jnp.where(seen, 1.0, 0.0).astype(low)
        gk_acc[...] = jnp.zeros_like(gk_acc)
        gq_acc[...] = jnp.zeros_like(gq_acc)

    v = v_ref[...]
    gm = gm_ref[...].astype(wide)
    gnum_wide = gm * recip_ref[...].astype(wide)
    gnum = gnum_wide.astype(low)
    product = gnum_wide * att_ref[...].astype(wide)
    high = product.astype(low)
    rest = (product - high.astype(wide)).astype(low)
    r = lax.broadcasted_iota(jnp.int32, (256, 128), 0)
    c = lax.broadcasted_iota(jnp.int32, (256, 128), 1)
    same_head = jnp.where(((r % 128) // 64) == (c // 64), 1.0, 0.0).astype(low)
    gtot = -dot(jnp.concatenate([high, rest], 1), same_head)
    gtot_high = gtot.astype(low)
    gtot_rest = (gtot - gtot_high.astype(wide)).astype(low)
    lane = lax.broadcasted_iota(jnp.int32, (1, 128), 1)
    left = jnp.concatenate([gnum, jnp.where(lane % 64 == 0, gtot_high, gtot_rest)], 1)
    gnum_half = gnum * jnp.asarray(0.5, low)
    queries, sides, gnums, keys = [], [], [], []
    for i in range(2):
        head = 2 * pair + i
        mine = lane_pick(heads, head * FEAT, (head + 1) * FEAT)
        queries.append(jnp.where(mine, q_ref[...], zero))
        keys.append(jnp.where(mine, k_ref[...], zero))
        lanes = lane_pick(128, 64 * i, 64 * i + 64)
        ones = jnp.where(lane_pick(128, 64 * i, 64 * i + 2), 1.0, 0.0).astype(low)
        sides.append(jnp.concatenate([jnp.where(lanes, v, zero), jnp.broadcast_to(ones, (length, 128))], 1))
        gnums.append(jnp.where(lanes, gnum_half, zero))
    for sb in range(0, length, TILE):
        n = sb + TILE
        gv = gconv_ref[sb:n, :].astype(wide)
        gk = None
        for i in range(2):
            one_plus = dot_nt(k_ref[sb:n, :], queries[i][sb:]) + 1.0
            mask = mask_ref[sb:n, sb:]
            kernel = (one_plus * one_plus + 1.0).astype(low) * mask
            gv = gv + dot(kernel, gnums[i][sb:])
            gkernel = dot_nt(sides[i][sb:n], left[sb:])
            gscores = (gkernel * one_plus).astype(low) * mask
            part = dot(gscores, queries[i][sb:])
            gk = part if gk is None else gk + part
            gq_acc[sb:, :] += dot_tn(gscores, keys[i][sb:n])
        gv_ref[sb:n, :] = gv.astype(low)
        gk_acc[sb:n, :] += gk

    @pl.when(pl.program_id(0) == pl.num_programs(0) - 1)
    def _():
        mine = slice(2 * FEAT * first, 2 * FEAT * first + gqk_ref.shape[1] // 2)
        gqk_ref[:, : gqk_ref.shape[1] // 2] = (gq_acc[:, mine] * FEAT ** (-0.5)).astype(low)
        gqk_ref[:, gqk_ref.shape[1] // 2 :] = gk_acc[:, mine].astype(low)


def attend_back(q, k, v, gm, att, recip, gconv, seg, first, count, onto=(), deps=()):
    length, width = v.shape
    heads = q.shape[1]
    column = pl.BlockSpec((length, 128), lambda p: (0, p + first))
    seg_row, seg_col = seg.reshape(1, length), seg.reshape(length, 1)
    return launch(
        functools.partial(attend_back_kernel, first),
        deps,
        onto,
        grid=(count,),
        in_specs=[whole(q), whole(k)] + [column] * 5 + [whole(seg_row), whole(seg_col)],
        out_specs=[pl.BlockSpec((length, 4 * FEAT * count), lambda p: (0, first // count)), column],
        out_shape=[jax.ShapeDtypeStruct((length, 2 * heads), low), jax.ShapeDtypeStruct((length, width), low)],
        scratch_shapes=[
            pltpu.VMEM((length, length), low),
            pltpu.VMEM((length, heads), wide),
            pltpu.VMEM((length, heads), wide),
        ],
        compiler_params=params(48),
        cost_estimate=cost(40 * count * 128 / width, 18),
        name="attention_backward",
    )(q, k, v, gm, att, recip, gconv, seg_row, seg_col)


def conv_back_kernel(v_ref, gm_ref, gate_ref, vec_ref, segc_ref, ggate_ref, gconv_ref, gfilt_ref):
    v_wide = v_ref[...].astype(wide)
    gm = gm_ref[...].astype(wide)
    seg = segc_ref[...]
    taps = [vec_ref[2 + j : 3 + j, :] for j in range(KW)]
    grad = gm * gate_ref[...].astype(wide)
    conv = taps[0] * v_wide
    gv_conv = taps[0] * grad
    lines = [jnp.sum(grad * v_wide, 0, keepdims=True)]
    for j in range(1, KW):
        moved = shift_rows(v_wide, seg, j, False)
        conv = conv + taps[j] * moved
        lines.append(jnp.sum(grad * moved, 0, keepdims=True))
        gv_conv = gv_conv + taps[j] * shift_rows(grad, seg, j, True)
    lines.append(jnp.zeros((LANES - KW, 128), wide))
    gfilt_ref[...] = jnp.concatenate(lines, 0).T.astype(low)
    ggate_ref[...] = (gm * conv).astype(low)
    gconv_ref[...] = gv_conv.astype(low)


def conv_back(v, gm, gate, vec, seg, deps=()):
    length, width = v.shape
    column = pl.BlockSpec((length, 128), lambda p: (0, p))
    small = pl.BlockSpec((8, 128), lambda p: (0, p))
    seg_col = seg.reshape(length, 1)
    return launch(
        conv_back_kernel,
        deps,
        grid=(width // 128,),
        in_specs=[column, column, column, small, whole(seg_col)],
        out_specs=[column, column, pl.BlockSpec((128, LANES), lambda p: (p, 0))],
        out_shape=[jax.ShapeDtypeStruct((length, width), low)] * 2 + [jax.ShapeDtypeStruct((width, LANES), low)],
        compiler_params=params(48),
        cost_estimate=cost(1, 10),
        name="convolution_backward",
    )(v, gm, gate, vec, seg_col)


def mix_kernel(x_ref, mixed_ref, vec_ref, weight_ref, middle_ref, hidden_ref):
    middle = x_ref[...].astype(wide) + dot(mixed_ref[...], weight_ref[...])
    inverse = lax.rsqrt(jnp.mean(middle * middle, axis=-1, keepdims=True) + EPS)
    middle_ref[...] = middle
    hidden_ref[...] = (middle * inverse * vec_ref[1:2, :]).astype(low)


def mix(x, mixed, vec, full, deps=()):
    length, width = x.shape
    return launch(
        mix_kernel,
        deps,
        grid=(length // TILE,),
        in_specs=[rows(TILE, width), rows(TILE, width), fixed(vec.shape), fixed((width, width))],
        out_specs=[rows(TILE, width), rows(TILE, width)],
        out_shape=[jax.ShapeDtypeStruct((length, width), wide), jax.ShapeDtypeStruct((length, width), low)],
        compiler_params=params(32),
        cost_estimate=cost(3, 16),
        name="mix",
    )(x, mixed, vec, full)


def first_half(n):
    return lambda i, *_: (jnp.minimum(i, n - 1), 0)


def second_half(n):
    return lambda i, *_: (jnp.maximum(i - n, 0), 0)


def feed_kernel(n, offs_ref, ha_ref, hb_ref, ca_ref, cb_ref, *refs):
    pieces, downs = refs[:4], refs[4:6]
    act_ref, both_ref, full_out_ref, down_out_ref, full_ref, down_ref, sems = refs[6:]
    copies = [
        pltpu.make_async_copy(full_ref, full_out_ref, sems.at[0]),
        pltpu.make_async_copy(down_ref, down_out_ref, sems.at[1]),
    ]
    step = pl.program_id(0)
    half = full_ref.shape[1] // 2

    @pl.when(step == 0)
    def _():
        place(offs_ref, FEED_AT, pieces, full_ref)
        place(offs_ref, DOWN_AT, downs, down_ref)
        for copy in copies:
            copy.start()

    def work(hidden, cotangent):
        for at in range(0, half, 256):
            gate = dot(hidden, full_ref[:, at : at + 256])
            up = dot(hidden, full_ref[:, half + at : half + at + 256])
            gact = dot_nt(cotangent, down_ref[at : at + 256, :])
            sig = jax.nn.sigmoid(gate)
            silu = gate * sig
            act_ref[:, at : at + 256] = (silu * up).astype(low)
            both_ref[:, at : at + 256] = (gact * up * (sig + silu * (1.0 - sig))).astype(low)
            both_ref[:, half + at : half + at + 256] = (gact * silu).astype(low)

    @pl.when(step < n)
    def _():
        work(ha_ref[...], ca_ref[...])

    @pl.when(step >= n)
    def _():
        work(hb_ref[...], cb_ref[...])

    @pl.when(step == 2 * n - 1)
    def _():
        for copy in copies:
            copy.wait()


def feed(offs, hidden, cotangent, j, w_down, pieces, down_pieces, deps=()):
    length, width = hidden[0].shape
    n = length // TILE
    half = w_down.shape[0]
    first = pl.BlockSpec((TILE, width), first_half(n))
    second = pl.BlockSpec((TILE, width), second_half(n))
    own_down = pl.BlockSpec((half // 2, width), lambda *_: (j, 0), pipeline_mode=pl.Buffered(1))
    given_rows = pl.BlockSpec(pieces[0].shape, lambda *_: (j, 0), pipeline_mode=pl.Buffered(1))
    return launch(
        functools.partial(feed_kernel, n),
        deps,
        scalars=1,
        grid=(2 * n,),
        in_specs=[first, second, first, second]
        + [fixed(pieces[0].shape), given_rows]
        + [fixed(p.shape) for p in pieces[2:]]
        + [own_down]
        + [fixed(p.shape) for p in down_pieces],
        out_specs=[rows(TILE, half), rows(TILE, 2 * half)] + [pl.BlockSpec(memory_space=pl.ANY)] * 2,
        scratch_shapes=[
            pltpu.VMEM((width, 2 * half), low),
            pltpu.VMEM((half, width), low),
            pltpu.SemaphoreType.DMA((2,)),
        ],
        out_shape=[
            jax.ShapeDtypeStruct((2 * length, half), low),
            jax.ShapeDtypeStruct((2 * length, 2 * half), low),
            jax.ShapeDtypeStruct((width, 2 * half), low),
            jax.ShapeDtypeStruct((half, width), low),
        ],
        compiler_params=params(48),
        cost_estimate=cost(16, 34),
        name="feed_in",
    )(offs, *hidden, *cotangent, *pieces, w_down, *down_pieces)


def weight_grad_kernel(shape_of, counts, outs, length, offs_ref, *refs):
    targets = [(ref, row * TILE) for ref, height in zip(refs[-len(outs) :], outs) for row in range(height)]
    step = pl.program_id(0)

    def work(lefts, rights):
        terms = max(len(lefts[0]), len(rights))

        def part_of(group, t):
            return group[t][...] if len(group) == terms else group[0][t * length : (t + 1) * length, :]

        for b, (ref, row) in enumerate(targets):
            value = None
            for t in range(terms):
                product = dot_tn(part_of(lefts[b], t), part_of(rights, t))
                value = product if value is None else value + product
            ref[row : row + TILE, :] = value.astype(low)

    start = 0
    for (left_at, right_at), count in zip(shape_of, counts):
        lefts = [[refs[n] for n in block] for block in left_at]
        rights = [refs[n] for n in right_at]
        if len(counts) == 1:
            work(lefts, rights)
        else:
            pl.when((step >= start) & (step < start + count))(functools.partial(work, lefts, rights))
        start += count


def weight_grad(offs, base, groups, outs, name, tile=512, deps=()):
    blocks = sum(outs)
    counts = [rights[0].shape[1] // tile for _, rights in groups]
    columns = sum(counts) * tile
    in_specs, operands, shape_of, known = [], [], [], {}
    start = 0
    for (lefts, rights), count in zip(groups, counts):
        key = tuple(id(a) for a in lefts)
        if key not in known:
            known[key] = []
            for b in range(blocks):
                known[key].append([len(operands) + n for n in range(len(lefts))])
                for a in lefts:
                    in_specs.append(pl.BlockSpec((a.shape[0], TILE), lambda j, offs, b=b: (0, offs[base + b])))
                    operands.append(a)
        shape_of.append((known[key], [len(operands) + n for n in range(len(rights))]))
        for a in rights:

            def where_to(j, offs, start=start, count=count):
                return (0, jnp.clip(j - start, 0, count - 1))

            in_specs.append(pl.BlockSpec((a.shape[0], tile), where_to))
            operands.append(a)
        start += count
    tokens = sum(a.shape[0] for a in groups[0][0])
    terms = max(len(groups[0][0]), len(groups[0][1]))
    return launch(
        functools.partial(weight_grad_kernel, shape_of, counts, outs, tokens // terms),
        deps,
        scalars=1,
        grid=(sum(counts),),
        in_specs=in_specs,
        out_specs=[pl.BlockSpec((height * TILE, tile), lambda j, offs: (0, j)) for height in outs],
        out_shape=[jax.ShapeDtypeStruct((height * TILE, columns), low) for height in outs],
        compiler_params=params(48, 48),
        cost_estimate=cost(2.5e-9 * tokens * 1024 * columns, (tokens * (1024 + columns) * 2 + 2048 * columns) / 2**20),
        name=name,
    )(offs, *operands)


def feed_back_kernel(a_ref, b_ref, wa_ref, wb_ref, out_ref):
    out_ref[...] = (dot_nt(a_ref[...], wa_ref[...]) + dot_nt(b_ref[...], wb_ref[...])).astype(low)


def feed_back(first, second, full_first, full_second, deps=()):
    length = first.shape[0] // 2
    width = full_first.shape[0]
    n = length // TILE
    tile = pl.BlockSpec((TILE, first.shape[1]), lambda i: (i + n, 0))
    return launch(
        feed_back_kernel,
        deps,
        grid=(n,),
        in_specs=[tile, tile, fixed(full_first.shape), fixed(full_second.shape)],
        out_specs=rows(TILE, width),
        out_shape=jax.ShapeDtypeStruct((length, width), low),
        compiler_params=params(32),
        cost_estimate=cost(10, 18),
        name="feed_back_partner",
    )(first, second, full_first, full_second)


def middle_back_kernel(
    a_ref, b_ref, other_ref, middle_ref, cot_ref, vec_ref, wa_ref, wb_ref, wo_ref,
    gmiddle_ref, gbranch_ref, gmixed_ref, ggain_ref,
):
    ghidden = dot_nt(a_ref[...], wa_ref[...]) + dot_nt(b_ref[...], wb_ref[...]) + other_ref[...].astype(wide)
    middle = middle_ref[...]
    inverse = lax.rsqrt(jnp.mean(middle * middle, axis=-1, keepdims=True) + EPS)
    normed = middle * inverse
    gain = jnp.sum(ghidden * normed, axis=0, keepdims=True)

    @pl.when(pl.program_id(0) == 0)
    def _():
        ggain_ref[...] = jnp.zeros_like(ggain_ref)

    ggain_ref[0:1, :] += gain
    scaled = ghidden * vec_ref[1:2, :]
    gmiddle = cot_ref[...].astype(wide) + inverse * (
        scaled - normed * jnp.mean(scaled * normed, axis=-1, keepdims=True)
    )
    gmiddle_ref[...] = gmiddle
    gbranch = gmiddle.astype(low)
    gbranch_ref[...] = gbranch
    gmixed_ref[...] = dot_nt(gbranch, wo_ref[...]).astype(low)


def middle_back(first, second, other, middle, cotangent, vec, full_first, full_second, w_output, deps=()):
    length, width = middle.shape
    tile = rows(TILE, first.shape[1])
    line = rows(TILE, width)
    return launch(
        middle_back_kernel,
        deps,
        grid=(length // TILE,),
        in_specs=[
            tile, tile, line, line, line, fixed(vec.shape), fixed(full_first.shape), fixed(full_second.shape), fixed((width, width))
        ],
        out_specs=[line, line, line, fixed((8, width))],
        out_shape=[
            jax.ShapeDtypeStruct((length, width), wide),
            jax.ShapeDtypeStruct((length, width), low),
            jax.ShapeDtypeStruct((length, width), low),
            jax.ShapeDtypeStruct((8, width), wide),
        ],
        compiler_params=params(48),
        cost_estimate=cost(13, 40),
        name="middle_back",
    )(first, second, other, middle, cotangent, vec, full_first, full_second, w_output)


def feed_out_kernel(add, *refs):
    out_ref = refs[-1]
    value = dot(refs[0][...], refs[2][...]) + dot(refs[1][...], refs[3][...])
    for ref in refs[4:-1]:
        value = value + ref[...].astype(wide)
    out_ref[...] = value.astype(low)


def feed_out(first, second, down_first, down_second, shift, extras, name, deps=()):
    length = first.shape[0] // 2
    width = down_first.shape[1]
    n = length // TILE
    tile = pl.BlockSpec((TILE, first.shape[1]), lambda i: (i + shift * n, 0))
    return launch(
        functools.partial(feed_out_kernel, len(extras)),
        deps,
        grid=(n,),
        in_specs=[tile, tile, fixed(down_first.shape), fixed(down_second.shape)] + [rows(TILE, width)] * len(extras),
        out_specs=rows(TILE, width),
        out_shape=jax.ShapeDtypeStruct((length, width), low),
        compiler_params=params(32),
        cost_estimate=cost(5, 16),
        name=name,
    )(first, second, down_first, down_second, *extras)


def tokens_back_kernel(gqk_ref, gv_ref, ggate_ref, x_ref, gmiddle_ref, vec_ref, full_ref, gtokens_ref, ggain_ref):
    two = gqk_ref.shape[1]
    width = x_ref.shape[1]
    quarter = two // 4
    ghidden = None
    for n, col in enumerate((0, 2, 1, 3)):
        at = width + col * quarter
        term = dot_nt(gqk_ref[:, n * quarter : (n + 1) * quarter], full_ref[:, at : at + quarter])
        ghidden = term if ghidden is None else ghidden + term
    ghidden = (
        ghidden
        + dot_nt(gv_ref[...], full_ref[:, width + two : 2 * width + two])
        + dot_nt(ggate_ref[...], full_ref[:, two + 2 * width : two + 3 * width])
    )
    x = x_ref[...].astype(wide)
    inverse = lax.rsqrt(jnp.mean(x * x, axis=-1, keepdims=True) + EPS)
    normed = x * inverse

    @pl.when(pl.program_id(0) == 0)
    def _():
        ggain_ref[...] = jnp.zeros_like(ggain_ref)

    ggain_ref[0:1, :] += jnp.sum(ghidden * normed, axis=0, keepdims=True)
    scaled = ghidden * vec_ref[0:1, :]
    gtokens_ref[...] = gmiddle_ref[...] + inverse * (
        scaled - normed * jnp.mean(scaled * normed, axis=-1, keepdims=True)
    )


def tokens_back(gqk, gv, ggate, x, gmiddle, vec, full, deps=()):
    length, width = x.shape
    line = rows(TILE, width)
    return launch(
        tokens_back_kernel,
        deps,
        grid=(length // TILE,),
        in_specs=[rows(TILE, gqk.shape[1]), line, line, line, line, fixed(vec.shape), fixed(full.shape)],
        out_specs=[line, fixed((8, width))],
        out_shape=[jax.ShapeDtypeStruct((length, width), wide), jax.ShapeDtypeStruct((8, width), wide)],
        compiler_params=params(40),
        cost_estimate=cost(7, 24),
        name="tokens_back",
    )(gqk, gv, ggate, x, gmiddle, vec, full)


def as_line(column):
    return jnp.broadcast_to(column, (column.shape[0], LANES)).T[0]


def spread_kernel(cols_ref, gain_ref, wg_ref, wu_ref, a_ref, b_ref, c_ref, d_ref, gate_ref, up_ref, ggain_ref):
    total = None
    for n, ref in enumerate((a_ref, b_ref, c_ref, d_ref)):
        quarter = ref.shape[1] // 4
        for part_y in range(2):
            at = pl.ds(pl.multiple_of(cols_ref[COLS_AT + 2 * n + part_y], 512), quarter)
            gate = ref[:, part_y * quarter : (part_y + 1) * quarter].astype(wide)
            up = ref[:, (2 + part_y) * quarter : (3 + part_y) * quarter].astype(wide)
            gate_ref[:, at] = gate
            up_ref[:, at] = up
            term = gate * wg_ref[:, at].astype(wide) + up * wu_ref[:, at].astype(wide)
            line = jnp.sum(term, axis=1, keepdims=True)
            total = line if total is None else total + line
    ggain_ref[...] = as_line(total / gain_ref[...])


def spread(cols, gain, w_gate, w_up, blocks, deps=()):
    height, width = blocks[0].shape
    shape = jax.ShapeDtypeStruct((height, 2 * width), wide)
    return launch(
        spread_kernel,
        deps,
        scalars=1,
        grid=(1,),
        in_specs=[fixed(gain.shape), fixed(w_gate.shape), fixed(w_up.shape)] + [fixed(b.shape) for b in blocks],
        out_specs=[fixed(shape.shape)] * 2 + [fixed(gain.shape[:1])],
        out_shape=[shape, shape, jax.ShapeDtypeStruct(gain.shape[:1], wide)],
        compiler_params=params(24),
        cost_estimate=cost(0.001, 16),
        name="spread",
    )(cols, gain, w_gate, w_up, *blocks)


def pack_kernel(at_ref, g1_ref, g2_ref, taps_ref, q_ref, k_ref, v_ref, c_ref, o_ref, pack_ref, part_ref):
    height = q_ref.shape[0]
    col = 0
    for ref in (o_ref, q_ref, k_ref, v_ref, c_ref):
        pack_ref[:, col : col + ref.shape[1]] = ref[...]
        col += ref.shape[1]
    small = jnp.concatenate([g1_ref[...].astype(wide)[None], g2_ref[...].astype(wide)[None], taps_ref[...].astype(wide)], 0)
    small = jnp.concatenate([small, jnp.zeros((LANES - small.shape[0], height), wide)], 0)
    pack_ref[:, col : col + LANES] = small.T.astype(low)
    size = part_ref.shape[0]
    part_ref[...] = pack_ref[pl.ds(pl.multiple_of(at_ref[QUARTER_AT] * size, 64), size), :]


def pack_mixer(at, gain_one, gain_two, taps, w_query, w_key, w_value, w_convgate, w_output):
    operands = (gain_one, gain_two, taps, w_query, w_key, w_value, w_convgate, w_output)
    height = w_query.shape[0]
    columns = sum(a.shape[1] for a in operands[3:]) + LANES
    shapes = [(height, columns), (height // 4, columns)]
    return launch(
        pack_kernel,
        scalars=1,
        grid=(1,),
        in_specs=[fixed(a.shape) for a in operands],
        out_specs=[fixed(a) for a in shapes],
        out_shape=[jax.ShapeDtypeStruct(a, low) for a in shapes],
        compiler_params=params(24),
        cost_estimate=cost(0.001, 4),
        name="pack_mixer",
    )(at, *operands)


def pack_feed_kernel(offs_ref, gate_ref, up_ref, down_ref, first_ref, second_ref, give_ref, *refs):
    send_refs, (low_ref, high_ref) = refs[:2], refs[2:]
    height = gate_ref.shape[0]
    sent = PACK_AT + 4 * offs_ref[X_AT]
    targets = (
        (first_ref, 0, PACK_AT),
        (second_ref, 0, PACK_AT + 2),
        (give_ref, 0, PACK_AT + 4),
        (give_ref, height, PACK_AT + 6),
        (send_refs[0], 0, sent),
        (send_refs[1], 0, sent + 2),
    )
    for ref, row, place_at in targets:
        quarter = ref.shape[1] // 4
        for part_y in range(2):
            at = pl.ds(pl.multiple_of(offs_ref[place_at + part_y], 512), quarter)
            ref[row : row + height, part_y * quarter : (part_y + 1) * quarter] = gate_ref[:, at]
            ref[row : row + height, (2 + part_y) * quarter : (3 + part_y) * quarter] = up_ref[:, at]
    size = low_ref.shape[0]
    low_ref[...] = down_ref[:size, :]
    high_ref[...] = down_ref[size:, :]


def pack_feed(offs, w_gate, w_up, w_down, deps=()):
    height, columns = w_gate.shape
    half = (height, columns // 2)
    shapes = [half, half, (2 * height, columns // 2), half, half] + [(w_down.shape[0] // 2, w_down.shape[1])] * 2
    return launch(
        pack_feed_kernel,
        deps,
        scalars=1,
        grid=(1,),
        in_specs=[fixed(w_gate.shape), fixed(w_up.shape), fixed(w_down.shape)],
        out_specs=[fixed(a) for a in shapes],
        out_shape=[jax.ShapeDtypeStruct(a, low) for a in shapes],
        compiler_params=params(24),
        cost_estimate=cost(0.001, 8),
        name="pack_feed",
    )(offs, w_gate, w_up, w_down)


STRIPS = 1


def operand_parts(operand):
    if not isinstance(operand, tuple):
        return operand, None, 1
    return operand if len(operand) == 3 else (*operand, 2)


def step(kernel, offs, operands, shapes, name, deps=(), giga=0.001):
    in_specs, arrays = [], []
    for operand in operands:
        array, half, parts = operand_parts(operand)
        height = array.shape[0] // parts

        def where_to(i, offs, half=half):
            if half is None:
                return (i, 0)
            return ((half(offs) if callable(half) else half) * STRIPS + i, 0)

        in_specs.append(pl.BlockSpec((height // STRIPS, array.shape[1]), where_to))
        arrays.append(array)
    return launch(
        kernel,
        deps,
        scalars=1,
        grid=(STRIPS,),
        in_specs=in_specs,
        out_specs=[rows(shape[0] // STRIPS, shape[1]) for shape in shapes],
        out_shape=[jax.ShapeDtypeStruct(shape, low) for shape in shapes],
        compiler_params=params(24),
        cost_estimate=cost(giga, 8),
        name=name,
    )(offs, *arrays)


def add(*refs):
    total = refs[0].astype(wide)
    for other in refs[1:]:
        total = total + other.astype(wide)
    return total.astype(low)


def sum_kernel(terms, offs_ref, *refs):
    for out_ref, groups in zip(refs[-len(terms) :], terms):
        col = 0
        for group in groups:
            width = refs[group[0]].shape[1]
            out_ref[:, col : col + width] = add(*(refs[n][...] for n in group))
            col += width


def strip_sum(offs, outputs, name, deps=()):
    operands, terms, shapes = [], [], []
    for groups in outputs:
        terms.append([])
        width = 0
        for group in groups:
            terms[-1].append(list(range(len(operands), len(operands) + len(group))))
            operands += group
            first, _, parts = operand_parts(group[0])
            height = first.shape[0] // parts
            width += first.shape[1]
        shapes.append((height, width))
    return step(functools.partial(sum_kernel, terms), offs, operands, shapes, name, deps)


def top_sum(offs, keep, came, deps=()):
    came = came if came.shape[0] * 2 == keep.shape[0] else (came, 0)
    return strip_sum(offs, [[[(keep, 0), came]]], "top_sum", deps)[0]


def rest_sum(offs, triples, deps=()):
    groups = []
    for keep, came, passed in triples:
        came = came if came.shape[0] * 2 == keep.shape[0] else (came, 1)
        groups.append([(keep, 1), came, passed])
    return strip_sum(offs, [groups], "rest_sum", deps)[0]


def halves_sum(offs, pairs, filters=None, deps=()):
    outputs = []
    for half in range(2):
        groups = [[(keep, half), (came, half)] for keep, came in pairs]
        if filters is not None:

            def quarter(offs_ref, half=half):
                return offs_ref[OWNER_AT + 2 + half]

            groups.append([(a, quarter, 4) for a in filters])
        outputs.append(groups)
    return strip_sum(offs, outputs, "halves_sum", deps)


def near_split(offs, keep, came, deps=()):
    def own(offs_ref):
        return offs_ref[X_AT]

    def other(offs_ref):
        return 1 - offs_ref[X_AT]

    return strip_sum(offs, [[[(keep, own), (came, own)]], [[(keep, other), (came, other)]]], "near_split", deps)


def pairs_sum(offs, pairs, deps=()):
    return strip_sum(offs, [[list(pair) for pair in pairs]], "pairs_sum", deps)[0]


def sort_kernel(offs_ref, total_ref, other_ref, own_ref, give_ref):
    skip = total_ref.shape[1] - own_ref.shape[1]

    @pl.when(offs_ref[X_AT + 1] == 0)
    def _():
        own_ref[...] = total_ref[:, skip:]
        give_ref[...] = other_ref[:, skip:]

    @pl.when(offs_ref[X_AT + 1] != 0)
    def _():
        own_ref[...] = other_ref[:, skip:]
        give_ref[...] = total_ref[:, skip:]


def sort_rows(offs, total, other, skip, deps=()):
    shape = (total.shape[0], total.shape[1] - skip)
    return step(sort_kernel, offs, [total, other], [shape, shape], "sort_rows", deps)


def settle_down_kernel(offs_ref, *refs):
    out_ref = refs[-1]
    size = out_ref.shape[0] // 4
    width = out_ref.shape[1]
    for n in range(4):
        side = offs_ref[X_AT] if n % 2 == 0 else 1 - offs_ref[X_AT]
        at = pl.ds(pl.multiple_of((n // 2) * 2 * size + side * size, 128), size)
        out_ref[at, :] = refs[n][:, :width].astype(wide)


def settle_down(offs, pairs, width, deps=()):
    operands = [a for pair in pairs for a in pair]
    size = operands[0].shape[0]
    column = pl.BlockSpec((size, width), lambda *_: (0, 0), pipeline_mode=pl.Buffered(1))
    return launch(
        settle_down_kernel,
        deps,
        scalars=1,
        grid=(1,),
        in_specs=[column] * 4,
        out_specs=fixed((4 * size, width)),
        out_shape=jax.ShapeDtypeStruct((4 * size, width), wide),
        compiler_params=params(24),
        cost_estimate=cost(0.001, 6),
        name="settle_down",
    )(offs, *operands)


def settle_mixer_kernel(
    offs_ref, gain_ref, mine_ref, other_ref, wq_ref, wk_ref, wv_ref, wc_ref,
    gq_ref, gk_ref, gv_ref, gc_ref, go_ref, gf_ref, ggain_ref, all_ref,
):
    size = mine_ref.shape[0]
    for ref, side in ((mine_ref, offs_ref[X_AT]), (other_ref, 1 - offs_ref[X_AT])):
        all_ref[pl.ds(pl.multiple_of(side * size, 128), size), :] = ref[...].astype(wide)
    width = wv_ref.shape[1]
    half = wq_ref.shape[1] // 2
    go_ref[...] = all_ref[:, :width]
    gc = all_ref[:, width : 2 * width]
    gc_ref[...] = gc
    gf_ref[...] = all_ref[:, 2 * width : 2 * width + LANES].T[:KW, :]
    at = 2 * width + LANES
    gv = all_ref[:, at + 4 * half :]
    gv_ref[...] = gv
    total = jnp.sum(gc * wc_ref[...].astype(wide), axis=1, keepdims=True)
    total = total + jnp.sum(gv * wv_ref[...].astype(wide), axis=1, keepdims=True)
    for n, (ref, weight_ref, cols) in enumerate(
        (
            (gq_ref, wq_ref, slice(0, half)),
            (gk_ref, wk_ref, slice(0, half)),
            (gq_ref, wq_ref, slice(half, 2 * half)),
            (gk_ref, wk_ref, slice(half, 2 * half)),
        )
    ):
        value = all_ref[:, at + n * half : at + (n + 1) * half]
        ref[:, cols] = value
        total = total + jnp.sum(value * weight_ref[:, cols].astype(wide), axis=1, keepdims=True)
    ggain_ref[...] = as_line(total / gain_ref[...])


def settle_mixer(offs, gain, mine, other, w_query, w_key, w_value, w_convgate, deps=()):
    operands = (gain, mine, other, w_query, w_key, w_value, w_convgate)
    height, width = w_value.shape
    shapes = [w_query.shape, w_key.shape, w_value.shape, w_convgate.shape, (height, width), (KW, height), gain.shape[:1]]
    return launch(
        settle_mixer_kernel,
        deps,
        scalars=1,
        grid=(1,),
        in_specs=[fixed(a.shape) for a in operands],
        out_specs=[fixed(a) for a in shapes],
        out_shape=[jax.ShapeDtypeStruct(a, wide) for a in shapes],
        scratch_shapes=[pltpu.VMEM((height, mine.shape[1]), wide)],
        compiler_params=params(24),
        cost_estimate=cost(0.001, 8),
        name="settle_mixer",
    )(offs, *operands)


def tick_kernel(offs_ref, out_ref):
    out_ref[...] = jnp.zeros_like(out_ref)


def tick(offs, deps=()):
    return launch(
        tick_kernel,
        deps,
        scalars=1,
        grid=(1,),
        in_specs=[],
        out_specs=fixed((16, LANES)),
        out_shape=jax.ShapeDtypeStruct((16, LANES), low),
        compiler_params=params(24),
        cost_estimate=cost(TICK, 8),
        name="arrived",
    )(offs)


def swap(value, axis):
    return lax.ppermute(value, axis, [(0, 1), (1, 0)])


def later(value, other):
    return lax.optimization_barrier((value, other))[0]


def part(value, index, count, axis=0):
    size = value.shape[axis] // count
    return lax.dynamic_slice_in_dim(value, index * size, size, axis)


def in_order(index, mine, other):
    return jnp.where(
        index == 0, jnp.concatenate([mine, other], 0), jnp.concatenate([other, mine], 0)
    )


def per_device(
    tokens, segment_ids, gain_one, w_query, w_key, w_value, w_convgate, w_output, conv_filter,
    gain_two, w_gate, w_up, w_down, cotangent,
):
    Order.last = None
    Order.scale = 0.05
    x = lax.axis_index("near")
    y = lax.axis_index("row")
    c = lax.axis_index("core")
    s = 2 * y + c
    width = tokens.shape[1]
    seg = segment_ids[0]
    block = w_down.shape[0]

    def flip(bits):
        return jnp.bitwise_xor(s, bits)

    small_block = block // 2
    z = lax.axis_index("far") % 2
    quarters = [(2 * a + b) * (SHARD_ROWS // 4) for a, b in ((x, z), (1 - x, z), (x, 1 - z), (1 - x, 1 - z))]

    def feed_cols(core, j):
        return [((2 * row + core) * 2 + j) * small_block for row in range(2)]

    feed_rows = [s, flip(1), jnp.bitwise_xor(flip(2), x), jnp.bitwise_xor(flip(3), x)]
    offs = [
        x,
        jnp.bitwise_xor(x, c),
        s * SHARD_ROWS,
        flip(1) * SHARD_ROWS,
        *(flip(2) * SHARD_ROWS + a for a in quarters),
        *(flip(3) * SHARD_ROWS + a for a in quarters),
        *(a * SHARD_ROWS for a in feed_rows),
        y * small_block,
        (1 - y) * small_block,
        0,
        0,
        *feed_cols(c, 0), *feed_cols(c, 1), *feed_cols(1 - c, 0), *feed_cols(1 - c, 1),
        *feed_cols(c, 0), *feed_cols(1 - c, 0), *feed_cols(c, 1), *feed_cols(1 - c, 1),
        2 * (1 - y) + 1 - x, 2 * (1 - y) + x, 2 * y + 1 - x, 2 * y + x,
        flip(3), flip(1), flip(2), s,
        2 * (1 - y) + 1 - x, 2 * y + 1 - x, 2 * (1 - y) + x, 2 * y + x,
        2 * x + z,
    ]
    offs = jnp.stack([jnp.asarray(a, jnp.int32) for a in offs])

    pack, pack_part = pack_mixer(
        offs, gain_one, gain_two, conv_filter, w_query, w_key, w_value, w_convgate, w_output
    )
    direct = swap(pack_part, "row")
    count = lax.axis_size("far")
    over_z = lax.ppermute(direct, "far", [(i, i ^ 1) for i in range(count)])
    came = [direct, swap(direct, "near"), over_z, swap(over_z, "near")]
    pack_pieces = [pack, swap(pack, "core"), *came, *(swap(a, "core") for a in came)]
    cot_other = swap(later(cotangent, direct), "core")

    mine_first, mine_second, give, *sends, down_first, down_second = pack_feed(offs, w_gate, w_up, w_down)
    given = swap(later(give, direct), "core")

    def across(value):
        pairs = []
        for side, row, core in np.ndindex(2, 2, 2):
            pairs.append((4 * side + 2 * row + core, 4 * side + 2 * (1 - row) + (core ^ side)))
        return lax.ppermute(value, ("near", "row", "core"), pairs)

    feed_pieces = [[own, given] for own in (mine_first, mine_second)]
    feed_pieces[0].append(across(later(sends[0], direct)))

    hidden_one, queries, keys, values, gates, vec, full_one = project(offs, tokens, pack_pieces, deps=[cot_other])
    feed_pieces[0].append(swap(later(feed_pieces[0][2], queries), "near"))
    down_pieces = [[swap(later(down_first, queries), "row")]]
    feed_pieces[1].append(across(later(sends[1], queries)))
    pairs = width // 256
    mixed, attention, recips = attend(queries, keys, values, gates, vec, seg, 0, 2 * pairs)
    middle, hidden_two = mix(tokens, mixed, vec, full_one, deps=[down_pieces[0][0]])
    down_pieces.append([swap(later(down_second, middle), "row")])
    tick(offs, [feed_pieces[0][3]])
    hiddens = [hidden_two, swap(hidden_two, "core")]
    cots = [cotangent, cot_other]

    Order.scale = 20.0

    def scatter_far(value):
        return lax.psum_scatter(value, "far", scatter_dimension=0, tiled=True)

    def gather_far(value):
        return lax.all_gather(later(value, tick(offs, [value])), "far", axis=0, tiled=True)

    def down_grad(act, deps=()):
        return weight_grad(offs, ACT_AT, [([act], cots)], (2, 2), "grad_down", deps=deps)

    def gate_grad(both):
        return weight_grad(offs, GRAD_AT, [(hiddens, [both])], (1, 1, 2), "grad_gate_up")

    first_feed = feed(offs, hiddens, cots, 0, w_down, feed_pieces[0], down_pieces[0])
    feed_pieces[1].append(swap(later(feed_pieces[1][2], first_feed[0]), "near"))
    down_send, down_keep = down_grad(first_feed[0], deps=[feed_pieces[1][2]])
    down_came = swap(down_send, "near")
    gate_send, gate_send_own, gate_keep = gate_grad(first_feed[1])
    gate_came, gate_came_own = swap(gate_send, "row"), swap(gate_send_own, "row")
    second_feed = feed(offs, hiddens, cots, 1, w_down, feed_pieces[1], down_pieces[1])
    acts, boths, fulls, downs = zip(first_feed, second_feed)
    down_passed = swap(top_sum(offs, down_keep, down_came), "row")
    gate_passed = swap(top_sum(offs, gate_keep, gate_came), "near")
    ghidden_part = feed_back(boths[0], boths[1], fulls[0], fulls[1])
    ghidden_other = swap(ghidden_part, "core")
    down_send_2, down_keep_2 = down_grad(second_feed[0])
    down_came_2 = swap(down_send_2, "near")
    gate_send_2, gate_send_own_2, gate_keep_2 = gate_grad(second_feed[1])
    gate_came_2, gate_came_own_2 = swap(gate_send_2, "row"), swap(gate_send_own_2, "row")
    feed_part = scatter_far(
        rest_sum(offs, [(down_keep, down_came, down_passed), (gate_keep, gate_came_own, gate_passed)])
    )
    tick(offs)
    gmiddle, gbranch, gmixed, _ = middle_back(
        boths[0], boths[1], ghidden_other, middle, cotangent, vec, fulls[0], fulls[1], full_one
    )
    down_passed_2 = swap(top_sum(offs, down_keep_2, down_came_2), "row")
    gate_passed_2 = swap(top_sum(offs, gate_keep_2, gate_came_2), "near")

    ggate, gconv, gfilter = conv_back(values, gmixed, gates, vec, seg)
    filter_came = swap(gfilter, "core")
    feed_sum = gather_far(feed_part)
    early_send, early_keep = weight_grad(
        offs, OWNER_AT, [([mixed], [gbranch]), ([hidden_one], [ggate])], (2, 2), "grad_output_convgate"
    )
    early_came = swap(early_send, "core")
    feed_part = scatter_far(
        rest_sum(
            offs, [(down_keep_2, down_came_2, down_passed_2), (gate_keep_2, gate_came_own_2, gate_passed_2)]
        )
    )
    tick(offs)
    attended = attend_back(queries, keys, values, gmixed, attention, recips, gconv, seg, 0, pairs)
    feed_other = swap(later(feed_sum, tick(offs, [feed_sum])), "near")
    early_give, early_held = halves_sum(offs, [(early_keep, early_came)], [gfilter, filter_came])
    early_came = swap(early_give, "row")
    gqk, gv = attend_back(
        queries, keys, values, gmixed, attention, recips, gconv, seg, pairs, pairs, onto=attended
    )
    late_send, late_keep = weight_grad(
        offs, OWNER_AT, [([hidden_one], [gqk]), ([hidden_one], [gv])], (2, 2), "grad_query_key_value"
    )
    late_came = swap(late_send, "core")
    early_own, early_other = near_split(offs, early_held, early_came)
    early_passed = swap(early_other, "near")
    feed_sum_2 = gather_far(feed_part)
    Order.scale = 0.05
    late_give, late_held = halves_sum(offs, [(late_keep, late_came)])
    late_came = swap(late_give, "row")
    own_rows, theirs = sort_rows(offs, feed_sum, feed_other, width)
    spreads = [own_rows, swap(theirs, "core")]
    out_part = feed_out(acts[0], acts[1], downs[0], downs[1], 1, [], "feed_out_partner")
    late_own, late_other = near_split(offs, late_held, late_came)
    late_passed = swap(late_other, "near")
    tick(offs, [feed_sum_2])
    mixer_near = pairs_sum(offs, [(early_own, early_passed), (late_own, late_passed)])
    feed_other_2 = swap(later(feed_sum_2, mixer_near), "near")
    Order.scale = 20.0
    mixer_sum = lax.psum(mixer_near, "far")
    out_came = swap(later(out_part, mixer_near), "core")
    tick(offs)
    result = feed_out(acts[0], acts[1], downs[0], downs[1], 0, [middle, out_came], "feed_out")
    grad_tokens, _ = tokens_back(gqk, gv, ggate, tokens, gmiddle, vec, full_one)
    own_rows, theirs = sort_rows(offs, feed_sum_2, feed_other_2, width)
    spreads += [own_rows, swap(theirs, "core")]
    grad_down = settle_down(offs, [(feed_sum, feed_other), (feed_sum_2, feed_other_2)], width)
    grad_gate, grad_up, ggain_two = spread(offs, gain_two[:, None].astype(wide), w_gate, w_up, spreads)
    mixer_other = swap(mixer_sum, "near")
    *grads, grad_output, grad_filter, ggain_one = settle_mixer(
        offs, gain_one[:, None].astype(wide), mixer_sum, mixer_other, w_query, w_key, w_value, w_convgate
    )
    return (
        result,
        grad_tokens,
        ggain_one,
        *grads,
        grad_output,
        grad_filter,
        ggain_two,
        grad_gate,
        grad_up,
        grad_down,
    )


def solution(mesh):
    replicas, shards = mesh.shape["rep"], mesh.shape["shard"]
    devices = np.asarray(mesh.devices).reshape(replicas // 2, 2, shards // 2, 2)
    fine = Mesh(devices, ("far", "near", "row", "core"))
    token = P(("far", "near", "row", "core"), None)
    line = P(("row", "core"))
    weight = P(("row", "core"), None)
    taps = P(None, ("row", "core"))
    return jax.shard_map(
        per_device,
        mesh=fine,
        in_specs=(
            token, token, line, weight, weight, weight, weight, weight, taps, line, weight, weight, weight, token
        ),
        out_specs=(
            token, token, line, weight, weight, weight, weight, weight, taps, line, weight, weight, weight
        ),
        check_vma=False,
    )
```

profile of v0, /device:TPU:0, one launch (start us, length us, event | category | flops | bytes accessed | tf_op | source)
XLA Modules:
  0.0 546.4 jit_solution(14079336330574892258)
XLA Ops:
  8.0 3.7 pack_mixer.1
  11.8 3.0 collective-permute-start.1
  14.7 11.1 %collective-permute-done.1.refs_4_ = bf16[64,3712]{1,0:T(8,128)(2,1)S(1)} collective-permute-done((bf16[64,3712]{1,0:T(8,128)(2,1)}, bf16[64,3712]{1,0:T(8,128)(2,1)S(1)}, u32[]{:S(2)}, u32[]{:S(2)}) %collective-permute-start.1) | collective-permute-done | bytes 475168 | tf_op jit(solution)/shard_map/ppermute | solution.py:1023
  29.6 7.4 %pack_feed.1 = (bf16[256,2048]{1,0:T(8,128)(2,1)}, bf16[256,2048]{1,0:T(8,128)(2,1)}, bf16[512,2048]{1,0:T(8,128)(2,1)}, bf16[256,2048]{1,0:T(8,128)(2,1)}, bf16...) custom-call(s32[49]{0:T(128)} %stack.149.refs_0_, bf16[256,4096]{1,0:T(8,128)(2,1)} %refs_2_.5, ...), custom_call_target="tpu_custom_call" | custom-call | flops 50000 | bytes 419430 | tf_op jit(solution)/shard_map/pack_feed/pallas_call | solution.py:61
  37.1 2.1 collective-permute-done.2.refs_5_
  42.2 11.3 %collective-permute-done.4.refs_7_ = bf16[64,3712]{1,0:T(8,128)(2,1)S(1)} collective-permute-done((bf16[64,3712]{1,0:T(8,128)(2,1)S(1)}, bf16[64,3712]{1,0:T(8,128)(2,1)S(1)}, u32[]{:S(2)}, u32[]{:S(2)}) %collective-permute-start.4) | collective-permute-done | bytes 475168 | tf_op jit(solution)/shard_map/ppermute | solution.py:1023
  56.9 12.7 %project.1 = (bf16[1024,1024]{1,0:T(8,128)(2,1)}, bf16[1024,256]{1,0:T(8,128)(2,1)}, bf16[1024,256]{1,0:T(8,128)(2,1)}, bf16[1024,1024]{1,0:T(8,128)(2,1)}, bf16...) custom-call(s32[49]{0:T(128)} %stack.149.refs_0_, bf16[1024,1024]{1,0:T(8,128)(2,1)} %refs_3_.10, ...), custom_call_target="tpu_custom_call" | custom-call | flops 350000000 | bytes 1153433 | tf_op jit(solution)/shard_map/project/pallas_call | solution.py:61
  74.0 20.5 %attention_forward.1 = (bf16[1024,1024]{1,0:T(8,128)(2,1)}, bf16[1024,1024]{1,0:T(8,128)(2,1)}, bf16[1024,1024]{1,0:T(8,128)(2,1)}) custom-call(bf16[1024,256]{1,0:T(8,128)(2,1)} %get-tuple-element.106.refs_0_, bf16[1024,256]{1,0:T(8,128)(2,1)} %get-tuple-element.107.refs_1_, bf16[1024,1024]{1,0:T(8,128)(2,1)} %get-tuple-element.108.refs_2_.refs_0_, ...), custom_call_target="tpu_custom_call" | custom-call | flops 900000000 | bytes 734003 | tf_op jit(solution)/shard_map/attention_forward/pallas_call | solution.py:61
  96.8 7.3 %mix.1 = (f32[1024,1024]{1,0:T(8,128)}, bf16[1024,1024]{1,0:T(8,128)(2,1)}) custom-call(bf16[1024,1024]{1,0:T(8,128)(2,1)} %refs_3_.10, bf16[1024,1024]{1,0:T(8,128)(2,1)} %get-tuple-element.112.refs_1_.refs_5_.refs_2_.refs_3_.refs_4_, f32[8,1024]{1,0:T(8,128)} %get-tuple-element.110.refs_4_.refs_2_.refs_5_.refs_3_, ...), custom_call_target="tpu_custom_call" | custom-call | flops 150000000 | bytes 838860 | tf_op jit(solution)/shard_map/mix/pallas_call | solution.py:61
  108.6 21.5 %feed_in.2 = (bf16[2048,1024]{1,0:T(8,128)(2,1)}, bf16[2048,2048]{1,0:T(8,128)(2,1)}, bf16[1024,2048]{1,0:T(8,128)(2,1)}, bf16[1024,1024]{1,0:T(8,128)(2,1)}) custom-call(s32[49]{0:T(128)} %stack.149.refs_0_, bf16[1024,1024]{1,0:T(8,128)(2,1)} %get-tuple-element.116.refs_1_.refs_3_.refs_5_.refs_7_, ...), custom_call_target="tpu_custom_call" | custom-call | flops 320000000000 | bytes 713031680 | tf_op jit(solution)/shard_map/feed_in/pallas_call | solution.py:61
  131.5 8.0 %grad_down.2 = (bf16[512,1024]{1,0:T(8,128)(2,1)}, bf16[512,1024]{1,0:T(8,128)(2,1)S(1)}) custom-call(s32[49]{0:T(128)S(1)} %copy-done.6, bf16[2048,1024]{1,0:T(8,128)(2,1)} %get-tuple-element.123.refs_1_.refs_2_.refs_3_.refs_4_.refs_8_.refs_0_, bf16[2048,1024]{1,0:T(8,128)(2,1)} %get-tuple-element.123.refs_1_.refs_2_.refs_3_.refs_4_.refs_8_.refs_0_, ...), custom_call_target="tpu_custom_call" | custom-call | flops 107374182400 | bytes 209715200 | tf_op jit(solution)/shard_map/grad_down/pallas_call | solution.py:61
  141.3 22.0 %grad_gate_up.2 = (bf16[256,2048]{1,0:T(8,128)(2,1)}, bf16[256,2048]{1,0:T(8,128)(2,1)}, bf16[512,2048]{1,0:T(8,128)(2,1)S(1)}) custom-call(s32[49]{0:T(128)S(1)} %copy-done.6, bf16[1024,1024]{1,0:T(8,128)(2,1)} %get-tuple-element.116.refs_1_.refs_3_.refs_5_.refs_7_, bf16[1024,1024]{1,0:T(8,128)(2,1)} %collective-permute-done.11.refs_2_.refs_4_.refs_6_.refs_8_, ...), custom_call_target="tpu_custom_call" | custom-call | flops 214748364800 | bytes 335544320 | tf_op jit(solution)/shard_map/grad_gate_up/pallas_call | solution.py:61
  166.7 21.4 %feed_in.3 = (bf16[2048,1024]{1,0:T(8,128)(2,1)}, bf16[2048,2048]{1,0:T(8,128)(2,1)}, bf16[1024,2048]{1,0:T(8,128)(2,1)}, bf16[1024,1024]{1,0:T(8,128)(2,1)}) custom-call(s32[49]{0:T(128)} %stack.149.refs_0_, bf16[1024,1024]{1,0:T(8,128)(2,1)} %get-tuple-element.116.refs_1_.refs_3_.refs_5_.refs_7_, ...), custom_call_target="tpu_custom_call" | custom-call | flops 320000000000 | bytes 713031680 | tf_op jit(solution)/shard_map/feed_in/pallas_call | solution.py:61
  188.1 2.8 top_sum.4.refs_3_
  191.4 22.1 %collective-permute-done.21.refs_2_ = bf16[256,2048]{1,0:T(8,128)(2,1)} collective-permute-done((bf16[256,2048]{1,0:T(8,128)(2,1)}, bf16[256,2048]{1,0:T(8,128)(2,1)}, u32[]{:S(2)}, u32[]{:S(2)}) %collective-permute-start.21) | collective-permute-done | bytes 1048608 | tf_op jit(solution)/shard_map/ppermute | solution.py:1023
  213.5 3.4 top_sum.5.refs_4_
  218.2 14.5 %feed_back_partner.1.refs_7_ = bf16[1024,1024]{1,0:T(8,128)(2,1)} custom-call(bf16[2048,2048]{1,0:T(8,128)(2,1)} %get-tuple-element.130.refs_9_.refs_0_, bf16[2048,2048]{1,0:T(8,128)(2,1)} %get-tuple-element.139.refs_1_.refs_9_, bf16[1024,2048]{1,0:T(8,128)(2,1)} %get-tuple-element.140.refs_2_.refs_6_, ...), custom_call_target="tpu_custom_call" | custom-call | flops 199999995904 | bytes 377487360 | tf_op jit(solution)/shard_map/feed_back_partner/pallas_call | solution.py:61
  232.7 8.1 %grad_down.3 = (bf16[512,1024]{1,0:T(8,128)(2,1)}, bf16[512,1024]{1,0:T(8,128)(2,1)S(1)}) custom-call(s32[49]{0:T(128)S(1)} %copy-done.7, bf16[2048,1024]{1,0:T(8,128)(2,1)} %get-tuple-element.133.refs_3_.refs_1_.refs_2_.refs_4_, bf16[2048,1024]{1,0:T(8,128)(2,1)} %get-tuple-element.133.refs_3_.refs_1_.refs_2_.refs_4_, ...), custom_call_target="tpu_custom_call" | custom-call | flops 107374182400 | bytes 209715200 | tf_op jit(solution)/shard_map/grad_down/pallas_call | solution.py:61
  242.5 13.5 %grad_gate_up.3 = (bf16[256,2048]{1,0:T(8,128)(2,1)}, bf16[256,2048]{1,0:T(8,128)(2,1)}, bf16[512,2048]{1,0:T(8,128)(2,1)S(1)}) custom-call(s32[49]{0:T(128)S(1)} %copy-done.7, bf16[1024,1024]{1,0:T(8,128)(2,1)} %get-tuple-element.116.refs_1_.refs_3_.refs_5_.refs_7_, bf16[1024,1024]{1,0:T(8,128)(2,1)} %collective-permute-done.11.refs_2_.refs_4_.refs_6_.refs_8_, ...), custom_call_target="tpu_custom_call" | custom-call | flops 214748364800 | bytes 335544320 | tf_op jit(solution)/shard_map/grad_gate_up/pallas_call | solution.py:61
  259.4 4.8 rest_sum.2.refs_1_
  265.5 20.6 %middle_back.1 = (f32[1024,1024]{1,0:T(8,128)}, bf16[1024,1024]{1,0:T(8,128)(2,1)}, bf16[1024,1024]{1,0:T(8,128)(2,1)}, f32[8,1024]{1,0:T(8,128)}) custom-call(bf16[2048,2048]{1,0:T(8,128)(2,1)} %get-tuple-element.130.refs_9_.refs_0_, bf16[2048,2048]{1,0:T(8,128)(2,1)} %get-tuple-element.139.refs_1_.refs_9_, ...), custom_call_target="tpu_custom_call" | custom-call | flops 260000006144 | bytes 838860800 | tf_op jit(solution)/shard_map/middle_back/pallas_call | solution.py:61
  286.1 2.8 top_sum.6.refs_3_
  289.1 3.4 top_sum.7.refs_5_
  292.6 1.8 collective-permute-start.28
  294.3 10.9 %convolution_backward.1 = (bf16[1024,1024]{1,0:T(8,128)(2,1)}, bf16[1024,1024]{1,0:T(8,128)(2,1)}, bf16[1024,128]{1,0:T(8,128)(2,1)}) custom-call(bf16[1024,1024]{1,0:T(8,128)(2,1)} %get-tuple-element.108.refs_2_.refs_0_, bf16[1024,1024]{1,0:T(8,128)(2,1)} %get-tuple-element.144.refs_1_.refs_3_, bf16[1024,1024]{1,0:T(8,128)(2,1)} %get-tuple-element.109.refs_3_.refs_2_, ...), custom_call_target="tpu_custom_call" | custom-call | flops 20000000000 | bytes 209715200 | tf_op jit(solution)/shard_map/convolution_backward/pallas_call | solution.py:61
  307.4 9.8 %grad_output_convgate.1 = (bf16[512,2048]{1,0:T(8,128)(2,1)}, bf16[512,2048]{1,0:T(8,128)(2,1)S(1)}) custom-call(s32[49]{0:T(128)S(1)} %copy-done.8, bf16[1024,1024]{1,0:T(8,128)(2,1)} %get-tuple-element.112.refs_1_.refs_5_.refs_2_.refs_3_.refs_4_, bf16[1024,1024]{1,0:T(8,128)(2,1)} %get-tuple-element.112.refs_1_.refs_5_.refs_2_.refs_3_.refs_4_, ...), custom_call_target="tpu_custom_call" | custom-call | flops 107374182400 | bytes 209715200 | tf_op jit(solution)/shard_map/grad_output_convgate/pallas_call | solution.py:61
  319.1 4.7 rest_sum.3.refs_1_
  325.2 21.2 %attention_backward.2 = (bf16[1024,512]{1,0:T(8,128)(2,1)}, bf16[1024,1024]{1,0:T(8,128)(2,1)}) custom-call(bf16[1024,256]{1,0:T(8,128)(2,1)} %get-tuple-element.106.refs_0_, bf16[1024,256]{1,0:T(8,128)(2,1)} %get-tuple-element.107.refs_1_, bf16[1024,1024]{1,0:T(8,128)(2,1)} %get-tuple-element.108.refs_2_.refs_0_, ...), custom_call_target="tpu_custom_call" | custom-call | flops 399999991808 | bytes 377487360 | tf_op jit(solution)/shard_map/attention_backward/pallas_call | solution.py:61
  347.6 4.5 halves_sum.2
  353.2 20.8 %attention_backward.3 = (bf16[1024,512]{1,0:T(8,128)(2,1)}, bf16[1024,1024]{1,0:T(8,128)(2,1)}) custom-call(bf16[1024,256]{1,0:T(8,128)(2,1)} %get-tuple-element.106.refs_0_, bf16[1024,256]{1,0:T(8,128)(2,1)} %get-tuple-element.107.refs_1_, bf16[1024,1024]{1,0:T(8,128)(2,1)} %get-tuple-element.108.refs_2_.refs_0_, ...), custom_call_target="tpu_custom_call", output_to_operand_aliasing={{0}: (9, {}), {1}: (10, {})} | custom-call | flops 399999991808 | bytes 377487360 | tf_op jit(solution)/shard_map/attention_backward/pallas_call | solution.py:61
  375.2 7.5 %grad_query_key_value.1 = (bf16[512,1536]{1,0:T(8,128)(2,1)}, bf16[512,1536]{1,0:T(8,128)(2,1)S(1)}) custom-call(s32[49]{0:T(128)S(1)} %copy-done.9, bf16[1024,1024]{1,0:T(8,128)(2,1)} %get-tuple-element.111.refs_7_.refs_6_.refs_8_.refs_9_.refs_1_.refs_2_.refs_3_.refs_4_, ...), custom_call_target="tpu_custom_call" | custom-call | flops 80530636800 | bytes 167772160 | tf_op jit(solution)/shard_map/grad_query_key_value/pallas_call | solution.py:61
  383.8 3.4 near_split.2
  389.6 3.8 halves_sum.3
  395.5 30.4 %collective-permute-done.29.refs_2_ = bf16[256,3072]{1,0:T(8,128)(2,1)S(1)} collective-permute-done((bf16[256,3072]{1,0:T(8,128)(2,1)S(1)}, bf16[256,3072]{1,0:T(8,128)(2,1)S(1)}, u32[]{:S(2)}, u32[]{:S(2)}) %collective-permute-start.29) | collective-permute-done | bytes 1572896 | tf_op jit(solution)/shard_map/ppermute | solution.py:1023
  427.0 4.0 sort_rows.2
  431.0 8.6 %feed_out_partner.1.refs_5_ = bf16[1024,1024]{1,0:T(8,128)(2,1)} custom-call(bf16[2048,1024]{1,0:T(8,128)(2,1)} %get-tuple-element.123.refs_1_.refs_2_.refs_3_.refs_4_.refs_8_.refs_0_, bf16[2048,1024]{1,0:T(8,128)(2,1)} %get-tuple-element.133.refs_3_.refs_1_.refs_2_.refs_4_, bf16[1024,1024]{1,0:T(8,128)(2,1)} %get-tuple-element.134.refs_2_, ...), custom_call_target="tpu_custom_call" | custom-call | flops 250000000 | bytes 838860 | tf_op jit(solution)/shard_map/feed_out_partner/pallas_call | solution.py:61
  439.6 3.0 near_split.3
  444.8 9.6 %collective-permute-done.36.refs_4_ = bf16[128,1536]{1,0:T(8,128)(2,1)} collective-permute-done((bf16[128,1536]{1,0:T(8,128)(2,1)}, bf16[128,1536]{1,0:T(8,128)(2,1)}, u32[]{:S(2)}, u32[]{:S(2)}) %collective-permute-start.36) | collective-permute-done | bytes 393248 | tf_op jit(solution)/shard_map/ppermute | solution.py:1023
  454.5 3.3 pairs_sum.1.refs_1_
  462.2 10.0 %feed_out.1.refs_7_ = bf16[1024,1024]{1,0:T(8,128)(2,1)} custom-call(bf16[2048,1024]{1,0:T(8,128)(2,1)} %get-tuple-element.123.refs_1_.refs_2_.refs_3_.refs_4_.refs_8_.refs_0_, bf16[2048,1024]{1,0:T(8,128)(2,1)} %get-tuple-element.133.refs_3_.refs_1_.refs_2_.refs_4_, bf16[1024,1024]{1,0:T(8,128)(2,1)} %get-tuple-element.134.refs_2_, ...), custom_call_target="tpu_custom_call" | custom-call | flops 99999997952 | bytes 335544320 | tf_op jit(solution)/shard_map/feed_out/pallas_call | solution.py:61
  472.2 14.5 %tokens_back.1 = (f32[1024,1024]{1,0:T(8,128)}, f32[8,1024]{1,0:T(8,128)}) custom-call(bf16[1024,512]{1,0:T(8,128)(2,1)} %get-tuple-element.162.refs_5_.refs_7_.refs_0_, bf16[1024,1024]{1,0:T(8,128)(2,1)} %get-tuple-element.163.refs_6_.refs_1_, bf16[1024,1024]{1,0:T(8,128)(2,1)} %get-tuple-element.148.refs_2_.refs_10_, bf16[1024,1024]{1,0:T(8,128)(2,1)} %refs_3_.10, ...), custom_call_target="tpu_custom_call" | custom-call | flops 140000002048 | bytes 503316480 | tf_op jit(solution)/shard_map/tokens_back/pallas_call | solution.py:61
  486.7 10.0 %collective-permute-done.40.refs_2_.refs_4_ = bf16[256,3072]{1,0:T(8,128)(2,1)} collective-permute-done((bf16[256,3072]{1,0:T(8,128)(2,1)}, bf16[256,3072]{1,0:T(8,128)(2,1)}, u32[]{:S(2)}, u32[]{:S(2)}) %collective-permute-start.40) | collective-permute-done | bytes 1572896 | tf_op jit(solution)/shard_map/ppermute | solution.py:1023
  496.8 4.0 sort_rows.3
  500.8 9.8 %all-reduce.2.cloned.1.call-done.refs_2_ = bf16[128,3712]{1,0:T(8,128)(2,1)} async-done(((bf16[128,3712]{1,0:T(8,128)(2,1)}), bf16[128,3712]{1,0:T(8,128)(2,1)}) %all-reduce.2.cloned.1.call-update) | async-done | bytes 950288 | tf_op jit(solution)/shard_map/psum | solution.py:1200
  513.7 4.5 settle_down.1.refs_8_
  519.2 8.5 %spread.1 = (f32[256,4096]{1,0:T(8,128)}, f32[256,4096]{1,0:T(8,128)}, f32[256]{0:T(256)}) custom-call(s32[49]{0:T(128)} %stack.149.refs_0_, f32[256,1]{1,0:T(8,128)} %copy.33.refs_1_, bf16[256,4096]{1,0:T(8,128)(2,1)} %refs_2_.5, bf16[256,4096]{1,0:T(8,128)(2,1)} %refs_3_.11, bf16[256,2048]{1,0:T(8,128)(2,1)} %get-tuple-element.169.refs_4_, ...), custom_call_target="tpu_custom_call" | custom-call | flops 20000000 | bytes 335544320 | tf_op jit(solution)/shard_map/spread/pallas_call | solution.py:61
  527.7 6.1 %collective-permute-done.38.refs_3_ = bf16[128,3712]{1,0:T(8,128)(2,1)S(1)} collective-permute-done((bf16[128,3712]{1,0:T(8,128)(2,1)}, bf16[128,3712]{1,0:T(8,128)(2,1)S(1)}, u32[]{:S(2)}, u32[]{:S(2)}) %collective-permute-start.38) | collective-permute-done | bytes 950304 | tf_op jit(solution)/shard_map/ppermute | solution.py:1023
  534.8 4.9 settle_mixer.1
  (167 shorter events, 64.4 us)
Async XLA Ops:
  7.2 298.1 %reduce-scatter.3.cloned.1.call-start = ((), (), s32[]{:S(2)}) async-start(), calls=%async_computation.2 | async-start | bytes 1966080 | tf_op jit(solution)/shard_map/reduce_scatter | solution.py:1124
  11.8 14.0 %collective-permute-start.1 = (bf16[64,3712]{1,0:T(8,128)(2,1)}, bf16[64,3712]{1,0:T(8,128)(2,1)S(1)}, u32[]{:S(2)}, u32[]{:S(2)}) collective-permute-start(bf16[64,3712]{1,0:T(8,128)(2,1)} %get-tuple-element.103), channel_id=1, source_target_pairs={{0,2},{2,0},{1,3},{3,1},{4,6},{6,4},{5,7},{7,5},{8,10},{10,8},{9,1... | collective-permute-start | bytes 1425416 | tf_op jit(solution)/shard_map/ppermute | solution.py:1023
  25.8 30.3 %collective-permute-start.9 = (bf16[1024,1024]{1,0:T(8,128)(2,1)S(1)}, bf16[1024,1024]{1,0:T(8,128)(2,1)}, u32[]{:S(2)}, u32[]{:S(2)}) collective-permute-start(bf16[1024,1024]{1,0:T(8,128)(2,1)S(1)} %copy-done.10), channel_id=1, source_target_pairs={{0,1},{1,0},{2,3},{3,2},{4,5},{5,4},{6,7},{7,6},{8,9},{9,8},{10,11... | collective-permute-start | bytes 6291464 | tf_op jit(solution)/shard_map/ppermute | solution.py:1023
  25.8 29.6 %collective-permute-start = (bf16[256,3712]{1,0:T(8,128)(2,1)}, bf16[256,3712]{1,0:T(8,128)(2,1)}, u32[]{:S(2)}, u32[]{:S(2)}) collective-permute-start(bf16[256,3712]{1,0:T(8,128)(2,1)} %get-tuple-element.102.refs_4_.refs_2_), channel_id=1, source_target_pairs={{0,1},{1,0},{2,3},{3,2},{4,5},{5,4},{6,7},{7,6},{8,9},{9,8},{10,11... | collective-permute-start | bytes 5701640 | tf_op jit(solution)/shard_map/ppermute | solution.py:1023
  26.3 12.8 %collective-permute-start.2 = (bf16[64,3712]{1,0:T(8,128)(2,1)S(1)}, bf16[64,3712]{1,0:T(8,128)(2,1)S(1)}, u32[]{:S(2)}, u32[]{:S(2)}) collective-permute-start(bf16[64,3712]{1,0:T(8,128)(2,1)S(1)} %collective-permute-done.1.refs_4_), channel_id=1, source_target_pairs={{0,4},{4,0},{1,5},{5,1},{2,6},{6,2},{3,7},{7,3},{8,12},{12,8},{9,1... | collective-permute-start | bytes 1425416 | tf_op jit(solution)/shard_map/ppermute | solution.py:1023
  28.0 12.9 %collective-permute-start.3 = (bf16[64,3712]{1,0:T(8,128)(2,1)S(1)}, bf16[64,3712]{1,0:T(8,128)(2,1)S(1)}, u32[]{:S(2)}, u32[]{:S(2)}) collective-permute-start(bf16[64,3712]{1,0:T(8,128)(2,1)S(1)} %collective-permute-done.1.refs_4_), channel_id=1, source_target_pairs={{0,8},{8,0},{16,24},{24,16},{1,9},{9,1},{17,25},{25,17},{2,10},{10... | collective-permute-start | bytes 1425416 | tf_op jit(solution)/shard_map/ppermute | solution.py:1092
  29.6 11.6 %collective-permute-start.5 = (bf16[64,3712]{1,0:T(8,128)(2,1)S(1)}, bf16[64,3712]{1,0:T(8,128)(2,1)S(1)}, u32[]{:S(2)}, u32[]{:S(2)}) collective-permute-start(bf16[64,3712]{1,0:T(8,128)(2,1)S(1)} %collective-permute-done.1.refs_4_), channel_id=1, source_target_pairs={{0,1},{1,0},{2,3},{3,2},{4,5},{5,4},{6,7},{7,6},{8,9},{9,8},{10,11... | collective-permute-start | bytes 1425416 | tf_op jit(solution)/shard_map/ppermute | solution.py:1023
  39.2 31.0 %collective-permute-start.13 = (bf16[256,2048]{1,0:T(8,128)(2,1)}, bf16[256,2048]{1,0:T(8,128)(2,1)}, u32[]{:S(2)}, u32[]{:S(2)}) collective-permute-start(bf16[256,2048]{1,0:T(8,128)(2,1)} %get-tuple-element.120), channel_id=1, source_target_pairs={{0,2},{1,3},{2,0},{3,1},{4,7},{5,6},{6,5},{7,4},{8,10},{9,11},{10,... | collective-permute-start | bytes 3145736 | tf_op jit(solution)/shard_map/ppermute | solution.py:1104
  40.9 12.6 %collective-permute-start.4 = (bf16[64,3712]{1,0:T(8,128)(2,1)S(1)}, bf16[64,3712]{1,0:T(8,128)(2,1)S(1)}, u32[]{:S(2)}, u32[]{:S(2)}) collective-permute-start(bf16[64,3712]{1,0:T(8,128)(2,1)S(1)} %collective-permute-done.3.refs_6_), channel_id=1, source_target_pairs={{0,4},{4,0},{1,5},{5,1},{2,6},{6,2},{3,7},{7,3},{8,12},{12,8},{9,1... | collective-permute-start | bytes 1425416 | tf_op jit(solution)/shard_map/ppermute | solution.py:1023
  41.2 12.3 %collective-permute-start.6 = (bf16[64,3712]{1,0:T(8,128)(2,1)S(1)}, bf16[64,3712]{1,0:T(8,128)(2,1)S(1)}, u32[]{:S(2)}, u32[]{:S(2)}) collective-permute-start(bf16[64,3712]{1,0:T(8,128)(2,1)S(1)} %collective-permute-done.2.refs_5_), channel_id=1, source_target_pairs={{0,1},{1,0},{2,3},{3,2},{4,5},{5,4},{6,7},{7,6},{8,9},{9,8},{10,11... | collective-permute-start | bytes 1425416 | tf_op jit(solution)/shard_map/ppermute | solution.py:1023
  53.6 1.8 collective-permute-start.7
  53.6 2.5 collective-permute-start.8
  69.6 26.3 %collective-permute-start.10 = (bf16[512,1024]{1,0:T(8,128)(2,1)}, bf16[512,1024]{1,0:T(8,128)(2,1)S(1)}, u32[]{:S(2)}, u32[]{:S(2)}) collective-permute-start(bf16[512,1024]{1,0:T(8,128)(2,1)} %get-tuple-element.115), channel_id=1, source_target_pairs={{0,2},{2,0},{1,3},{3,1},{4,6},{6,4},{5,7},{7,5},{8,10},{10,8},{9,1... | collective-permute-start | bytes 3145736 | tf_op jit(solution)/shard_map/ppermute | solution.py:1023
  70.2 34.5 %collective-permute-start.14 = (bf16[256,2048]{1,0:T(8,128)(2,1)}, bf16[256,2048]{1,0:T(8,128)(2,1)S(1)}, u32[]{:S(2)}, u32[]{:S(2)}) collective-permute-start(bf16[256,2048]{1,0:T(8,128)(2,1)} %collective-permute-done.13.refs_7_), channel_id=1, source_target_pairs={{0,4},{4,0},{1,5},{5,1},{2,6},{6,2},{3,7},{7,3},{8,12},{12,8},{9,1... | collective-permute-start | bytes 3145736 | tf_op jit(solution)/shard_map/ppermute | solution.py:1023
  72.9 34.0 %collective-permute-start.12 = (bf16[512,2048]{1,0:T(8,128)(2,1)}, bf16[512,2048]{1,0:T(8,128)(2,1)}, u32[]{:S(2)}, u32[]{:S(2)}) collective-permute-start(bf16[512,2048]{1,0:T(8,128)(2,1)} %get-tuple-element.118), channel_id=1, source_target_pairs={{0,1},{1,0},{2,3},{3,2},{4,5},{5,4},{6,7},{7,6},{8,9},{9,8},{10,11... | collective-permute-start | bytes 6291464 | tf_op jit(solution)/shard_map/ppermute | solution.py:1023
  72.9 57.2 %collective-permute-start.15 = (bf16[256,2048]{1,0:T(8,128)(2,1)}, bf16[256,2048]{1,0:T(8,128)(2,1)}, u32[]{:S(2)}, u32[]{:S(2)}) collective-permute-start(bf16[256,2048]{1,0:T(8,128)(2,1)} %get-tuple-element.126), channel_id=1, source_target_pairs={{0,2},{1,3},{2,0},{3,1},{4,7},{5,6},{6,5},{7,4},{8,10},{9,11},{10,... | collective-permute-start | bytes 3145736 | tf_op jit(solution)/shard_map/ppermute | solution.py:1104
  104.1 4.5 collective-permute-start.11
  104.1 62.5 %collective-permute-start.17 = (bf16[512,1024]{1,0:T(8,128)(2,1)}, bf16[512,1024]{1,0:T(8,128)(2,1)}, u32[]{:S(2)}, u32[]{:S(2)}) collective-permute-start(bf16[512,1024]{1,0:T(8,128)(2,1)} %get-tuple-element.129), channel_id=1, source_target_pairs={{0,2},{2,0},{1,3},{3,1},{4,6},{6,4},{5,7},{7,5},{8,10},{10,8},{9,1... | collective-permute-start | bytes 3145736 | tf_op jit(solution)/shard_map/ppermute | solution.py:1023
  130.2 36.5 %collective-permute-start.16 = (bf16[256,2048]{1,0:T(8,128)(2,1)}, bf16[256,2048]{1,0:T(8,128)(2,1)}, u32[]{:S(2)}, u32[]{:S(2)}) collective-permute-start(bf16[256,2048]{1,0:T(8,128)(2,1)} %collective-permute-done.15.refs_7_), channel_id=1, source_target_pairs={{0,4},{4,0},{1,5},{5,1},{2,6},{6,2},{3,7},{7,3},{8,12},{12,8},{9,1... | collective-permute-start | bytes 3145736 | tf_op jit(solution)/shard_map/ppermute | solution.py:1023
  140.5 47.5 %collective-permute-start.18 = (bf16[512,1024]{1,0:T(8,128)(2,1)}, bf16[512,1024]{1,0:T(8,128)(2,1)}, u32[]{:S(2)}, u32[]{:S(2)}) collective-permute-start(bf16[512,1024]{1,0:T(8,128)(2,1)} %get-tuple-element.131.refs_10_), channel_id=1, source_target_pairs={{0,4},{4,0},{1,5},{5,1},{2,6},{6,2},{3,7},{7,3},{8,12},{12,8},{9,1... | collective-permute-start | bytes 3145736 | tf_op jit(solution)/shard_map/ppermute | solution.py:1023
  164.6 92.7 %collective-permute-start.20 = (bf16[256,2048]{1,0:T(8,128)(2,1)}, bf16[256,2048]{1,0:T(8,128)(2,1)}, u32[]{:S(2)}, u32[]{:S(2)}) collective-permute-start(bf16[256,2048]{1,0:T(8,128)(2,1)} %get-tuple-element.138), channel_id=1, source_target_pairs={{0,2},{2,0},{1,3},{3,1},{4,6},{6,4},{5,7},{7,5},{8,10},{10,8},{9,1... | collective-permute-start | bytes 3145736 | tf_op jit(solution)/shard_map/ppermute | solution.py:1023
  165.1 48.4 %collective-permute-start.21 = (bf16[256,2048]{1,0:T(8,128)(2,1)}, bf16[256,2048]{1,0:T(8,128)(2,1)}, u32[]{:S(2)}, u32[]{:S(2)}) collective-permute-start(bf16[256,2048]{1,0:T(8,128)(2,1)} %get-tuple-element.132.refs_11_), channel_id=1, source_target_pairs={{0,2},{2,0},{1,3},{3,1},{4,6},{6,4},{5,7},{7,5},{8,10},{10,8},{9,1... | collective-permute-start | bytes 3145736 | tf_op jit(solution)/shard_map/ppermute | solution.py:1023
  190.9 67.0 %collective-permute-start.19 = (bf16[256,1024]{1,0:T(8,128)(2,1)}, bf16[256,1024]{1,0:T(8,128)(2,1)}, u32[]{:S(2)}, u32[]{:S(2)}) collective-permute-start(bf16[256,1024]{1,0:T(8,128)(2,1)} %top_sum.4.refs_3_), channel_id=1, source_target_pairs={{0,2},{2,0},{1,3},{3,1},{4,6},{6,4},{5,7},{7,5},{8,10},{10,8},{9,1... | collective-permute-start | bytes 1572872 | tf_op jit(solution)/shard_map/ppermute | solution.py:1023
  216.9 42.5 %collective-permute-start.22 = (bf16[256,2048]{1,0:T(8,128)(2,1)}, bf16[256,2048]{1,0:T(8,128)(2,1)}, u32[]{:S(2)}, u32[]{:S(2)}) collective-permute-start(bf16[256,2048]{1,0:T(8,128)(2,1)} %top_sum.5.refs_4_), channel_id=1, source_target_pairs={{0,4},{4,0},{1,5},{5,1},{2,6},{6,2},{3,7},{7,3},{8,12},{12,8},{9,1... | collective-permute-start | bytes 3145736 | tf_op jit(solution)/shard_map/ppermute | solution.py:1023
  232.7 32.8 %collective-permute-start.23 = (bf16[1024,1024]{1,0:T(8,128)(2,1)}, bf16[1024,1024]{1,0:T(8,128)(2,1)}, u32[]{:S(2)}, u32[]{:S(2)}) collective-permute-start(bf16[1024,1024]{1,0:T(8,128)(2,1)} %feed_back_partner.1.refs_7_), channel_id=1, source_target_pairs={{0,1},{1,0},{2,3},{3,2},{4,5},{5,4},{6,7},{7,6},{8,9},{9,8},{10,11... | collective-permute-start | bytes 6291464 | tf_op jit(solution)/shard_map/ppermute | solution.py:1023
  241.7 44.4 %collective-permute-start.25 = (bf16[512,1024]{1,0:T(8,128)(2,1)}, bf16[512,1024]{1,0:T(8,128)(2,1)}, u32[]{:S(2)}, u32[]{:S(2)}) collective-permute-start(bf16[512,1024]{1,0:T(8,128)(2,1)} %get-tuple-element.142.refs_10_), channel_id=1, source_target_pairs={{0,4},{4,0},{1,5},{5,1},{2,6},{6,2},{3,7},{7,3},{8,12},{12,8},{9,1... | collective-permute-start | bytes 3145736 | tf_op jit(solution)/shard_map/ppermute | solution.py:1023
  257.3 31.8 %collective-permute-start.24 = (bf16[256,2048]{1,0:T(8,128)(2,1)}, bf16[256,2048]{1,0:T(8,128)(2,1)}, u32[]{:S(2)}, u32[]{:S(2)}) collective-permute-start(bf16[256,2048]{1,0:T(8,128)(2,1)} %get-tuple-element.143.refs_7_), channel_id=1, source_target_pairs={{0,2},{2,0},{1,3},{3,1},{4,6},{6,4},{5,7},{7,5},{8,10},{10,8},{9,1... | collective-permute-start | bytes 3145736 | tf_op jit(solution)/shard_map/ppermute | solution.py:1023
  257.9 61.2 %collective-permute-start.27 = (bf16[256,2048]{1,0:T(8,128)(2,1)}, bf16[256,2048]{1,0:T(8,128)(2,1)}, u32[]{:S(2)}, u32[]{:S(2)}) collective-permute-start(bf16[256,2048]{1,0:T(8,128)(2,1)} %get-tuple-element.153), channel_id=1, source_target_pairs={{0,2},{2,0},{1,3},{3,1},{4,6},{6,4},{5,7},{7,5},{8,10},{10,8},{9,1... | collective-permute-start | bytes 3145736 | tf_op jit(solution)/shard_map/ppermute | solution.py:1023
  264.2 82.2 %all-gather.3.cloned.1.call-start = ((), (), s32[]{:S(2)}) async-start(), calls=%async_computation.3 | async-start | bytes 1966080 | tf_op jit(solution)/shard_map/all_gather | solution.py:1127
  288.9 30.2 %collective-permute-start.26 = (bf16[256,1024]{1,0:T(8,128)(2,1)}, bf16[256,1024]{1,0:T(8,128)(2,1)}, u32[]{:S(2)}, u32[]{:S(2)}) collective-permute-start(bf16[256,1024]{1,0:T(8,128)(2,1)} %top_sum.6.refs_3_), channel_id=1, source_target_pairs={{0,2},{2,0},{1,3},{3,1},{4,6},{6,4},{5,7},{7,5},{8,10},{10,8},{9,1... | collective-permute-start | bytes 1572872 | tf_op jit(solution)/shard_map/ppermute | solution.py:1023
  292.6 26.5 %collective-permute-start.28 = (bf16[256,2048]{1,0:T(8,128)(2,1)}, bf16[256,2048]{1,0:T(8,128)(2,1)}, u32[]{:S(2)}, u32[]{:S(2)}) collective-permute-start(bf16[256,2048]{1,0:T(8,128)(2,1)} %top_sum.7.refs_5_), channel_id=1, source_target_pairs={{0,4},{4,0},{1,5},{5,1},{2,6},{6,2},{3,7},{7,3},{8,12},{12,8},{9,1... | collective-permute-start | bytes 3145736 | tf_op jit(solution)/shard_map/ppermute | solution.py:1023
  305.2 42.4 %collective-permute-start.31 = (bf16[1024,128]{1,0:T(8,128)(2,1)}, bf16[1024,128]{1,0:T(8,128)(2,1)}, u32[]{:S(2)}, u32[]{:S(2)}) collective-permute-start(bf16[1024,128]{1,0:T(8,128)(2,1)} %get-tuple-element.160.refs_3_.refs_7_), channel_id=1, source_target_pairs={{0,1},{1,0},{2,3},{3,2},{4,5},{5,4},{6,7},{7,6},{8,9},{9,8},{10,11... | collective-permute-start | bytes 786440 | tf_op jit(solution)/shard_map/ppermute | solution.py:1023
  306.6 80.5 %reduce-scatter.5.cloned.1.call-start = ((), (), s32[]{:S(2)}) async-start(), calls=%async_computation.4 | async-start | bytes 1966080 | tf_op jit(solution)/shard_map/reduce_scatter | solution.py:1124
  318.5 29.1 %collective-permute-start.30 = (bf16[512,2048]{1,0:T(8,128)(2,1)}, bf16[512,2048]{1,0:T(8,128)(2,1)}, u32[]{:S(2)}, u32[]{:S(2)}) collective-permute-start(bf16[512,2048]{1,0:T(8,128)(2,1)} %get-tuple-element.155.refs_7_), channel_id=1, source_target_pairs={{0,1},{1,0},{2,3},{3,2},{4,5},{5,4},{6,7},{7,6},{8,9},{9,8},{10,11... | collective-permute-start | bytes 6291464 | tf_op jit(solution)/shard_map/ppermute | solution.py:1023
  325.1 118.5 %all-gather.5.cloned.1.call-start = ((), (), s32[]{:S(2)}) async-start(), calls=%async_computation.5 | async-start | bytes 1966080 | tf_op jit(solution)/shard_map/all_gather | solution.py:1127
  352.1 31.7 %collective-permute-start.33 = (bf16[256,2176]{1,0:T(8,128)(2,1)}, bf16[256,2176]{1,0:T(8,128)(2,1)}, u32[]{:S(2)}, u32[]{:S(2)}) collective-permute-start(bf16[256,2176]{1,0:T(8,128)(2,1)} %get-tuple-element.161.refs_11_), channel_id=1, source_target_pairs={{0,2},{2,0},{1,3},{3,1},{4,6},{6,4},{5,7},{7,5},{8,10},{10,8},{9,1... | collective-permute-start | bytes 3342344 | tf_op jit(solution)/shard_map/ppermute | solution.py:1023
  383.8 5.8 %collective-permute-start.32 = (bf16[512,1536]{1,0:T(8,128)(2,1)}, bf16[512,1536]{1,0:T(8,128)(2,1)}, u32[]{:S(2)}, u32[]{:S(2)}) collective-permute-start(bf16[512,1536]{1,0:T(8,128)(2,1)} %get-tuple-element.165.refs_5_), channel_id=1, source_target_pairs={{0,1},{1,0},{2,3},{3,2},{4,5},{5,4},{6,7},{7,6},{8,9},{9,8},{10,11... | collective-permute-start | bytes 4718600 | tf_op jit(solution)/shard_map/ppermute | solution.py:1023
  388.6 37.3 %collective-permute-start.29 = (bf16[256,3072]{1,0:T(8,128)(2,1)S(1)}, bf16[256,3072]{1,0:T(8,128)(2,1)S(1)}, u32[]{:S(2)}, u32[]{:S(2)}) collective-permute-start(bf16[256,3072]{1,0:T(8,128)(2,1)S(1)} %copy-done.15), channel_id=1, source_target_pairs={{0,4},{4,0},{1,5},{5,1},{2,6},{6,2},{3,7},{7,3},{8,12},{12,8},{9,1... | collective-permute-start | bytes 4718600 | tf_op jit(solution)/shard_map/ppermute | solution.py:1023
  393.5 46.2 %collective-permute-start.35 = (bf16[256,1536]{1,0:T(8,128)(2,1)}, bf16[256,1536]{1,0:T(8,128)(2,1)}, u32[]{:S(2)}, u32[]{:S(2)}) collective-permute-start(bf16[256,1536]{1,0:T(8,128)(2,1)} %get-tuple-element.168.refs_3_), channel_id=1, source_target_pairs={{0,2},{2,0},{1,3},{3,1},{4,6},{6,4},{5,7},{7,5},{8,10},{10,8},{9,1... | collective-permute-start | bytes 2359304 | tf_op jit(solution)/shard_map/ppermute | solution.py:1023
  393.8 51.1 %collective-permute-start.34 = (bf16[128,2176]{1,0:T(8,128)(2,1)}, bf16[128,2176]{1,0:T(8,128)(2,1)}, u32[]{:S(2)}, u32[]{:S(2)}) collective-permute-start(bf16[128,2176]{1,0:T(8,128)(2,1)} %get-tuple-element.170), channel_id=1, source_target_pairs={{0,4},{4,0},{1,5},{5,1},{2,6},{6,2},{3,7},{7,3},{8,12},{12,8},{9,1... | collective-permute-start | bytes 1671176 | tf_op jit(solution)/shard_map/ppermute | solution.py:1023
  431.0 87.1 %collective-permute-start.39 = (bf16[256,2048]{1,0:T(8,128)(2,1)}, bf16[256,2048]{1,0:T(8,128)(2,1)}, u32[]{:S(2)}, u32[]{:S(2)}) collective-permute-start(bf16[256,2048]{1,0:T(8,128)(2,1)} %get-tuple-element.177), channel_id=1, source_target_pairs={{0,1},{1,0},{2,3},{3,2},{4,5},{5,4},{6,7},{7,6},{8,9},{9,8},{10,11... | collective-permute-start | bytes 3145736 | tf_op jit(solution)/shard_map/ppermute | solution.py:1023
  442.6 11.8 %collective-permute-start.36 = (bf16[128,1536]{1,0:T(8,128)(2,1)}, bf16[128,1536]{1,0:T(8,128)(2,1)}, u32[]{:S(2)}, u32[]{:S(2)}) collective-permute-start(bf16[128,1536]{1,0:T(8,128)(2,1)} %get-tuple-element.173), channel_id=1, source_target_pairs={{0,4},{4,0},{1,5},{5,1},{2,6},{6,2},{3,7},{7,3},{8,12},{12,8},{9,1... | collective-permute-start | bytes 1179656 | tf_op jit(solution)/shard_map/ppermute | solution.py:1023
  457.7 4.5 collective-permute-start.37
  459.0 51.6 %all-reduce.2.cloned.1.call-start = ((), (), s32[]{:S(2)}) async-start(), calls=%async_computation.6 | async-start | bytes 1900544 | tf_op jit(solution)/shard_map/psum | solution.py:1200
  459.6 37.2 %collective-permute-start.40 = (bf16[256,3072]{1,0:T(8,128)(2,1)}, bf16[256,3072]{1,0:T(8,128)(2,1)}, u32[]{:S(2)}, u32[]{:S(2)}) collective-permute-start(bf16[256,3072]{1,0:T(8,128)(2,1)} %all-gather.5.cloned.1.call-done.refs_1_.refs_3_), channel_id=1, source_target_pairs={{0,4},{4,0},{1,5},{5,1},{2,6},{6,2},{3,7},{7,3},{8,12},{12,8},{9,1... | collective-permute-start | bytes 4718600 | tf_op jit(solution)/shard_map/ppermute | solution.py:1023
  486.7 25.4 %copy-start.30 = (bf16[256]{0:T(256)(128)(2,1)S(1)}, bf16[256]{0:T(256)(128)(2,1)}, u32[]{:S(2)}) copy-start(bf16[256]{0:T(256)(128)(2,1)} %refs_2_.3) | copy-start | bytes 1540
  500.8 17.4 %collective-permute-start.41 = (bf16[256,2048]{1,0:T(8,128)(2,1)}, bf16[256,2048]{1,0:T(8,128)(2,1)S(1)}, u32[]{:S(2)}, u32[]{:S(2)}) collective-permute-start(bf16[256,2048]{1,0:T(8,128)(2,1)} %get-tuple-element.180), channel_id=1, source_target_pairs={{0,1},{1,0},{2,3},{3,2},{4,5},{5,4},{6,7},{7,6},{8,9},{9,8},{10,11... | collective-permute-start | bytes 3145736 | tf_op jit(solution)/shard_map/ppermute | solution.py:1023
  510.6 23.2 %collective-permute-start.38 = (bf16[128,3712]{1,0:T(8,128)(2,1)}, bf16[128,3712]{1,0:T(8,128)(2,1)S(1)}, u32[]{:S(2)}, u32[]{:S(2)}) collective-permute-start(bf16[128,3712]{1,0:T(8,128)(2,1)} %all-reduce.2.cloned.1.call-done.refs_2_), channel_id=1, source_target_pairs={{0,4},{4,0},{1,5},{5,1},{2,6},{6,2},{3,7},{7,3},{8,12},{12,8},{9,1... | collective-permute-start | bytes 2850824 | tf_op jit(solution)/shard_map/ppermute | solution.py:1023
  (31 other events, 239.4 us)
Sparse Core Ops, SparseCore 0:
  264.3 35.7 reduce-scatter.2
  306.7 37.5 all-gather.2
  346.7 34.1 reduce-scatter.4
  388.7 37.0 all-gather.4
  461.9 48.6 all-reduce.1
where the time goes:
time: 553 us; the launch traced here: 546 us
  Pallas kernels  361 us (65%)
  waiting for transfers between devices  120 us (22%)
  starting transfers between devices  33.2 us (6%)
  local copies, waits for them, and re-layouts  18.2 us (3%)
  between operations  14.4 us (3%)
    pallas_call x45, Pallas kernels, call(): result = run(*operands, *deps)  361 us
    ppermute x39, waiting for transfers between devices, swap(): return lax.ppermute(value, axis, [(0, 1), (1, 0)])  110 us
    ppermute x39, starting transfers between devices, swap(): return lax.ppermute(value, axis, [(0, 1), (1, 0)])  28.7 us
    unnamed x64, local copies, waits for them, and re-layouts  14.8 us
  transfers between devices with their start and end apart: 47, of which 14 were waited for; matrix products, arithmetic and copies ran while one was open for 0% of the time, Pallas kernels for 64%

commit v1 on v0

--- a/solution.py
+++ b/solution.py
@@ -1137,8 +1137,9 @@
     down_send, down_keep = down_grad(first_feed[0], deps=[feed_pieces[1][2]])
     down_came = swap(down_send, "near")
     gate_send, gate_send_own, gate_keep = gate_grad(first_feed[1])
-    gate_came, gate_came_own = swap(gate_send, "row"), swap(gate_send_own, "row")
+    gate_came = swap(gate_send, "row")
     second_feed = feed(offs, hiddens, cots, 1, w_down, feed_pieces[1], down_pieces[1])
+    gate_came_own = swap(later(gate_send_own, second_feed[0]), "row")
     acts, boths, fulls, downs = zip(first_feed, second_feed)
     down_passed = swap(top_sum(offs, down_keep, down_came), "row")
     gate_passed = swap(top_sum(offs, gate_keep, gate_came), "near")
@@ -1147,11 +1148,11 @@
     down_send_2, down_keep_2 = down_grad(second_feed[0])
     down_came_2 = swap(down_send_2, "near")
     gate_send_2, gate_send_own_2, gate_keep_2 = gate_grad(second_feed[1])
-    gate_came_2, gate_came_own_2 = swap(gate_send_2, "row"), swap(gate_send_own_2, "row")
+    gate_came_2 = swap(gate_send_2, "row")
     feed_part = scatter_far(
         rest_sum(offs, [(down_keep, down_came, down_passed), (gate_keep, gate_came_own, gate_passed)])
     )
-    tick(offs)
+    gate_came_own_2 = swap(later(gate_send_own_2, tick(offs)), "row")
     gmiddle, gbranch, gmixed, _ = middle_back(
         boths[0], boths[1], ghidden_other, middle, cotangent, vec, fulls[0], fulls[1], full_one
     )
@@ -1182,14 +1183,14 @@
         offs, OWNER_AT, [([hidden_one], [gqk]), ([hidden_one], [gv])], (2, 2), "grad_query_key_value"
     )
     late_came = swap(late_send, "core")
+    own_rows, theirs = sort_rows(offs, feed_sum, feed_other, width)
+    spreads = [own_rows, swap(theirs, "core")]
     early_own, early_other = near_split(offs, early_held, early_came)
     early_passed = swap(early_other, "near")
     feed_sum_2 = gather_far(feed_part)
     Order.scale = 0.05
     late_give, late_held = halves_sum(offs, [(late_keep, late_came)])
     late_came = swap(late_give, "row")
-    own_rows, theirs = sort_rows(offs, feed_sum, feed_other, width)
-    spreads = [own_rows, swap(theirs, "core")]
     out_part = feed_out(acts[0], acts[1], downs[0], downs[1], 1, [], "feed_out_partner")
     late_own, late_other = near_split(offs, late_held, late_came)
     late_passed = swap(late_other, "near")

time: 553 us -> 542 us (0.980)
  waiting for transfers between devices: 120 us -> 106 us
    ppermute x39, waiting for transfers between devices: 110 us -> 79.2 us  [swap(): return lax.ppermute(value, axis, [(0, 1), (1, 0)])]
    all_gather x2, waiting for transfers between devices: 0.01 us -> 17.2 us  [gather_far(): lax.all_gather(later(value, tick(offs, [value])), 'far', axis=0, tiled=True)]
    unnamed x64 -> x66, local copies, waits for them, and re-layouts: 14.8 us -> 15.7 us
  transfers between devices with their start and end apart: 47 -> 47, of which waited for: 14 -> 15; matrix products, arithmetic and copies ran while one was open for 0% -> 0% of each run, Pallas kernels for 64% -> 66%
where the time goes in v1:
time: 542 us; the launch traced here: 536 us
  Pallas kernels  360 us (66%)
  waiting for transfers between devices  106 us (20%)
  starting transfers between devices  36.1 us (7%)
  local copies, waits for them, and re-layouts  19 us (4%)
  between operations  14.4 us (3%)
    pallas_call x45, Pallas kernels, call(): result = run(*operands, *deps)  360 us
    ppermute x39, waiting for transfers between devices, swap(): return lax.ppermute(value, axis, [(0, 1), (1, 0)])  79.2 us
    ppermute x39, starting transfers between devices, swap(): return lax.ppermute(value, axis, [(0, 1), (1, 0)])  31.6 us
    all_gather x2, waiting for transfers between devices, gather_far(): lax.all_gather(later(value, tick(offs, [value])), 'far', axis=0, tiled=True)  17.2 us
    unnamed x66, local copies, waits for them, and re-layouts  15.7 us
  transfers between devices with their start and end apart: 47, of which 15 were waited for; matrix products, arithmetic and copies ran while one was open for 0% of the time, Pallas kernels for 66%

profile of v1, /device:TPU:0, one launch (start us, length us, event | category | flops | bytes accessed | tf_op | source)
XLA Modules:
  0.0 536.0 jit_solution(5973262128160246904)
XLA Ops:
  8.0 3.7 pack_mixer.1
  11.7 3.0 collective-permute-start.1
  14.7 11.1 %collective-permute-done.1.refs_4_ = bf16[64,3712]{1,0:T(8,128)(2,1)S(1)} collective-permute-done((bf16[64,3712]{1,0:T(8,128)(2,1)}, bf16[64,3712]{1,0:T(8,128)(2,1)S(1)}, u32[]{:S(2)}, u32[]{:S(2)}) %collective-permute-start.1) | collective-permute-done | bytes 475168 | tf_op jit(solution)/shard_map/ppermute | solution.py:1023
  29.6 7.4 %pack_feed.1 = (bf16[256,2048]{1,0:T(8,128)(2,1)}, bf16[256,2048]{1,0:T(8,128)(2,1)}, bf16[512,2048]{1,0:T(8,128)(2,1)}, bf16[256,2048]{1,0:T(8,128)(2,1)}, bf16...) custom-call(s32[49]{0:T(128)} %stack.149.refs_0_, bf16[256,4096]{1,0:T(8,128)(2,1)} %refs_2_.5, ...), custom_call_target="tpu_custom_call" | custom-call | flops 50000 | bytes 419430 | tf_op jit(solution)/shard_map/pack_feed/pallas_call | solution.py:61
  37.0 2.1 collective-permute-done.2.refs_5_
  42.2 11.3 %collective-permute-done.4.refs_7_ = bf16[64,3712]{1,0:T(8,128)(2,1)S(1)} collective-permute-done((bf16[64,3712]{1,0:T(8,128)(2,1)S(1)}, bf16[64,3712]{1,0:T(8,128)(2,1)S(1)}, u32[]{:S(2)}, u32[]{:S(2)}) %collective-permute-start.4) | collective-permute-done | bytes 475168 | tf_op jit(solution)/shard_map/ppermute | solution.py:1023
  56.8 12.7 %project.1 = (bf16[1024,1024]{1,0:T(8,128)(2,1)}, bf16[1024,256]{1,0:T(8,128)(2,1)}, bf16[1024,256]{1,0:T(8,128)(2,1)}, bf16[1024,1024]{1,0:T(8,128)(2,1)}, bf16...) custom-call(s32[49]{0:T(128)} %stack.149.refs_0_, bf16[1024,1024]{1,0:T(8,128)(2,1)} %refs_3_.10, ...), custom_call_target="tpu_custom_call" | custom-call | flops 350000000 | bytes 1153433 | tf_op jit(solution)/shard_map/project/pallas_call | solution.py:61
  74.0 20.5 %attention_forward.1 = (bf16[1024,1024]{1,0:T(8,128)(2,1)}, bf16[1024,1024]{1,0:T(8,128)(2,1)}, bf16[1024,1024]{1,0:T(8,128)(2,1)}) custom-call(bf16[1024,256]{1,0:T(8,128)(2,1)} %get-tuple-element.108.refs_0_, bf16[1024,256]{1,0:T(8,128)(2,1)} %get-tuple-element.109.refs_1_, bf16[1024,1024]{1,0:T(8,128)(2,1)} %get-tuple-element.110.refs_2_.refs_0_, ...), custom_call_target="tpu_custom_call" | custom-call | flops 900000000 | bytes 734003 | tf_op jit(solution)/shard_map/attention_forward/pallas_call | solution.py:61
  96.8 7.3 %mix.1 = (f32[1024,1024]{1,0:T(8,128)}, bf16[1024,1024]{1,0:T(8,128)(2,1)}) custom-call(bf16[1024,1024]{1,0:T(8,128)(2,1)} %refs_3_.10, bf16[1024,1024]{1,0:T(8,128)(2,1)} %get-tuple-element.114.refs_1_.refs_5_.refs_2_.refs_3_.refs_4_, f32[8,1024]{1,0:T(8,128)} %get-tuple-element.112.refs_4_.refs_2_.refs_5_.refs_3_, ...), custom_call_target="tpu_custom_call" | custom-call | flops 150000000 | bytes 838860 | tf_op jit(solution)/shard_map/mix/pallas_call | solution.py:61
  108.6 21.5 %feed_in.2 = (bf16[2048,1024]{1,0:T(8,128)(2,1)}, bf16[2048,2048]{1,0:T(8,128)(2,1)}, bf16[1024,2048]{1,0:T(8,128)(2,1)}, bf16[1024,1024]{1,0:T(8,128)(2,1)}) custom-call(s32[49]{0:T(128)} %stack.149.refs_0_, bf16[1024,1024]{1,0:T(8,128)(2,1)} %get-tuple-element.118.refs_1_.refs_3_.refs_5_.refs_7_, ...), custom_call_target="tpu_custom_call" | custom-call | flops 320000000000 | bytes 713031680 | tf_op jit(solution)/shard_map/feed_in/pallas_call | solution.py:61
  131.5 8.0 %grad_down.2 = (bf16[512,1024]{1,0:T(8,128)(2,1)}, bf16[512,1024]{1,0:T(8,128)(2,1)S(1)}) custom-call(s32[49]{0:T(128)S(1)} %copy-done.6, bf16[2048,1024]{1,0:T(8,128)(2,1)} %get-tuple-element.125.refs_1_.refs_2_.refs_3_.refs_4_.refs_8_.refs_0_, bf16[2048,1024]{1,0:T(8,128)(2,1)} %get-tuple-element.125.refs_1_.refs_2_.refs_3_.refs_4_.refs_8_.refs_0_, ...), custom_call_target="tpu_custom_call" | custom-call | flops 107374182400 | bytes 209715200 | tf_op jit(solution)/shard_map/grad_down/pallas_call | solution.py:61
  141.3 22.0 %grad_gate_up.2 = (bf16[256,2048]{1,0:T(8,128)(2,1)}, bf16[256,2048]{1,0:T(8,128)(2,1)}, bf16[512,2048]{1,0:T(8,128)(2,1)S(1)}) custom-call(s32[49]{0:T(128)S(1)} %copy-done.6, bf16[1024,1024]{1,0:T(8,128)(2,1)} %get-tuple-element.118.refs_1_.refs_3_.refs_5_.refs_7_, bf16[1024,1024]{1,0:T(8,128)(2,1)} %collective-permute-done.11.refs_2_.refs_4_.refs_6_.refs_8_, ...), custom_call_target="tpu_custom_call" | custom-call | flops 214748364800 | bytes 335544320 | tf_op jit(solution)/shard_map/grad_gate_up/pallas_call | solution.py:61
  165.1 21.4 %feed_in.3 = (bf16[2048,1024]{1,0:T(8,128)(2,1)}, bf16[2048,2048]{1,0:T(8,128)(2,1)}, bf16[1024,2048]{1,0:T(8,128)(2,1)}, bf16[1024,1024]{1,0:T(8,128)(2,1)}) custom-call(s32[49]{0:T(128)} %stack.149.refs_0_, bf16[1024,1024]{1,0:T(8,128)(2,1)} %get-tuple-element.118.refs_1_.refs_3_.refs_5_.refs_7_, ...), custom_call_target="tpu_custom_call" | custom-call | flops 320000000000 | bytes 713031680 | tf_op jit(solution)/shard_map/feed_in/pallas_call | solution.py:61
  186.5 2.8 top_sum.4.refs_3_
  190.8 3.4 top_sum.5.refs_4_
  195.5 14.5 %feed_back_partner.1.refs_7_ = bf16[1024,1024]{1,0:T(8,128)(2,1)} custom-call(bf16[2048,2048]{1,0:T(8,128)(2,1)} %get-tuple-element.132.refs_9_.refs_0_, bf16[2048,2048]{1,0:T(8,128)(2,1)} %get-tuple-element.138.refs_1_.refs_9_, bf16[1024,2048]{1,0:T(8,128)(2,1)} %get-tuple-element.139.refs_2_.refs_6_, ...), custom_call_target="tpu_custom_call" | custom-call | flops 199999995904 | bytes 377487360 | tf_op jit(solution)/shard_map/feed_back_partner/pallas_call | solution.py:61
  211.0 8.0 %grad_down.3 = (bf16[512,1024]{1,0:T(8,128)(2,1)}, bf16[512,1024]{1,0:T(8,128)(2,1)S(1)}) custom-call(s32[49]{0:T(128)S(1)} %copy-done.7, bf16[2048,1024]{1,0:T(8,128)(2,1)} %get-tuple-element.135.refs_3_.refs_1_.refs_2_.refs_4_, bf16[2048,1024]{1,0:T(8,128)(2,1)} %get-tuple-element.135.refs_3_.refs_1_.refs_2_.refs_4_, ...), custom_call_target="tpu_custom_call" | custom-call | flops 107374182400 | bytes 209715200 | tf_op jit(solution)/shard_map/grad_down/pallas_call | solution.py:61
  220.3 13.5 %grad_gate_up.3 = (bf16[256,2048]{1,0:T(8,128)(2,1)}, bf16[256,2048]{1,0:T(8,128)(2,1)}, bf16[512,2048]{1,0:T(8,128)(2,1)S(1)}) custom-call(s32[49]{0:T(128)S(1)} %copy-done.7, bf16[1024,1024]{1,0:T(8,128)(2,1)} %get-tuple-element.118.refs_1_.refs_3_.refs_5_.refs_7_, bf16[1024,1024]{1,0:T(8,128)(2,1)} %collective-permute-done.11.refs_2_.refs_4_.refs_6_.refs_8_, ...), custom_call_target="tpu_custom_call" | custom-call | flops 214748364800 | bytes 335544320 | tf_op jit(solution)/shard_map/grad_gate_up/pallas_call | solution.py:61
  236.7 4.8 rest_sum.2.refs_1_
  243.3 20.4 %middle_back.1 = (f32[1024,1024]{1,0:T(8,128)}, bf16[1024,1024]{1,0:T(8,128)(2,1)}, bf16[1024,1024]{1,0:T(8,128)(2,1)}, f32[8,1024]{1,0:T(8,128)}) custom-call(bf16[2048,2048]{1,0:T(8,128)(2,1)} %get-tuple-element.132.refs_9_.refs_0_, bf16[2048,2048]{1,0:T(8,128)(2,1)} %get-tuple-element.138.refs_1_.refs_9_, ...), custom_call_target="tpu_custom_call" | custom-call | flops 260000006144 | bytes 838860800 | tf_op jit(solution)/shard_map/middle_back/pallas_call | solution.py:61
  263.7 2.8 top_sum.6.refs_3_
  268.0 3.4 top_sum.7.refs_5_
  272.7 10.9 %convolution_backward.1 = (bf16[1024,1024]{1,0:T(8,128)(2,1)}, bf16[1024,1024]{1,0:T(8,128)(2,1)}, bf16[1024,128]{1,0:T(8,128)(2,1)}) custom-call(bf16[1024,1024]{1,0:T(8,128)(2,1)} %get-tuple-element.110.refs_2_.refs_0_, bf16[1024,1024]{1,0:T(8,128)(2,1)} %get-tuple-element.147.refs_1_.refs_3_, bf16[1024,1024]{1,0:T(8,128)(2,1)} %get-tuple-element.111.refs_3_.refs_2_, ...), custom_call_target="tpu_custom_call" | custom-call | flops 20000000000 | bytes 209715200 | tf_op jit(solution)/shard_map/convolution_backward/pallas_call | solution.py:61
  285.7 9.9 %grad_output_convgate.1 = (bf16[512,2048]{1,0:T(8,128)(2,1)}, bf16[512,2048]{1,0:T(8,128)(2,1)S(1)}) custom-call(s32[49]{0:T(128)S(1)} %copy-done.8, bf16[1024,1024]{1,0:T(8,128)(2,1)} %get-tuple-element.114.refs_1_.refs_5_.refs_2_.refs_3_.refs_4_, bf16[1024,1024]{1,0:T(8,128)(2,1)} %get-tuple-element.114.refs_1_.refs_5_.refs_2_.refs_3_.refs_4_, ...), custom_call_target="tpu_custom_call" | custom-call | flops 107374182400 | bytes 209715200 | tf_op jit(solution)/shard_map/grad_output_convgate/pallas_call | solution.py:61
  297.5 4.7 rest_sum.3.refs_1_
  303.5 21.3 %attention_backward.2 = (bf16[1024,512]{1,0:T(8,128)(2,1)}, bf16[1024,1024]{1,0:T(8,128)(2,1)}) custom-call(bf16[1024,256]{1,0:T(8,128)(2,1)} %get-tuple-element.108.refs_0_, bf16[1024,256]{1,0:T(8,128)(2,1)} %get-tuple-element.109.refs_1_, bf16[1024,1024]{1,0:T(8,128)(2,1)} %get-tuple-element.110.refs_2_.refs_0_, ...), custom_call_target="tpu_custom_call" | custom-call | flops 399999991808 | bytes 377487360 | tf_op jit(solution)/shard_map/attention_backward/pallas_call | solution.py:61
  324.8 9.7 %all-gather.3.cloned.1.call-done.refs_1_ = bf16[256,3072]{1,0:T(8,128)(2,1)} async-done(((bf16[64,3072]{1,0:T(8,128)(2,1)}), bf16[256,3072]{1,0:T(8,128)(2,1)}) %all-gather.3.cloned.1.call-update) | async-done | bytes 1572880 | tf_op jit(solution)/shard_map/all_gather | solution.py:1127
  335.8 4.5 halves_sum.2
  341.8 20.9 %attention_backward.3 = (bf16[1024,512]{1,0:T(8,128)(2,1)}, bf16[1024,1024]{1,0:T(8,128)(2,1)}) custom-call(bf16[1024,256]{1,0:T(8,128)(2,1)} %get-tuple-element.108.refs_0_, bf16[1024,256]{1,0:T(8,128)(2,1)} %get-tuple-element.109.refs_1_, bf16[1024,1024]{1,0:T(8,128)(2,1)} %get-tuple-element.110.refs_2_.refs_0_, ...), custom_call_target="tpu_custom_call", output_to_operand_aliasing={{0}: (9, {}), {1}: (10, {})} | custom-call | flops 399999991808 | bytes 377487360 | tf_op jit(solution)/shard_map/attention_backward/pallas_call | solution.py:61
  365.5 7.5 %grad_query_key_value.1 = (bf16[512,1536]{1,0:T(8,128)(2,1)}, bf16[512,1536]{1,0:T(8,128)(2,1)S(1)}) custom-call(s32[49]{0:T(128)S(1)} %copy-done.9, bf16[1024,1024]{1,0:T(8,128)(2,1)} %get-tuple-element.113.refs_7_.refs_6_.refs_8_.refs_9_.refs_1_.refs_2_.refs_3_.refs_4_, ...), custom_call_target="tpu_custom_call" | custom-call | flops 80530636800 | bytes 167772160 | tf_op jit(solution)/shard_map/grad_query_key_value/pallas_call | solution.py:61
  374.1 24.6 %collective-permute-done.33.refs_2_ = bf16[256,3072]{1,0:T(8,128)(2,1)S(1)} collective-permute-done((bf16[256,3072]{1,0:T(8,128)(2,1)S(1)}, bf16[256,3072]{1,0:T(8,128)(2,1)S(1)}, u32[]{:S(2)}, u32[]{:S(2)}) %collective-permute-start.33) | collective-permute-done | bytes 1572896 | tf_op jit(solution)/shard_map/ppermute | solution.py:1023
  399.8 4.0 sort_rows.2
  403.8 3.4 near_split.2
  408.4 3.9 halves_sum.3
  414.3 8.7 %feed_out_partner.1.refs_5_ = bf16[1024,1024]{1,0:T(8,128)(2,1)} custom-call(bf16[2048,1024]{1,0:T(8,128)(2,1)} %get-tuple-element.125.refs_1_.refs_2_.refs_3_.refs_4_.refs_8_.refs_0_, bf16[2048,1024]{1,0:T(8,128)(2,1)} %get-tuple-element.135.refs_3_.refs_1_.refs_2_.refs_4_, bf16[1024,1024]{1,0:T(8,128)(2,1)} %get-tuple-element.136.refs_2_, ...), custom_call_target="tpu_custom_call" | custom-call | flops 250000000 | bytes 838860 | tf_op jit(solution)/shard_map/feed_out_partner/pallas_call | solution.py:61
  423.0 7.7 %collective-permute-done.35.refs_2_.refs_4_ = bf16[256,1536]{1,0:T(8,128)(2,1)S(1)} collective-permute-done((bf16[256,1536]{1,0:T(8,128)(2,1)}, bf16[256,1536]{1,0:T(8,128)(2,1)S(1)}, u32[]{:S(2)}, u32[]{:S(2)}) %collective-permute-start.35) | collective-permute-done | bytes 786464 | tf_op jit(solution)/shard_map/ppermute | solution.py:1023
  431.6 3.0 near_split.3
  436.2 7.5 %all-gather.5.cloned.1.call-done.refs_1_.refs_3_ = bf16[256,3072]{1,0:T(8,128)(2,1)} async-done(((bf16[64,3072]{1,0:T(8,128)(2,1)}), bf16[256,3072]{1,0:T(8,128)(2,1)}) %all-gather.5.cloned.1.call-update) | async-done | bytes 1572880 | tf_op jit(solution)/shard_map/all_gather | solution.py:1127
  445.0 3.2 pairs_sum.1.refs_1_
  452.7 10.0 %feed_out.1.refs_7_ = bf16[1024,1024]{1,0:T(8,128)(2,1)} custom-call(bf16[2048,1024]{1,0:T(8,128)(2,1)} %get-tuple-element.125.refs_1_.refs_2_.refs_3_.refs_4_.refs_8_.refs_0_, bf16[2048,1024]{1,0:T(8,128)(2,1)} %get-tuple-element.135.refs_3_.refs_1_.refs_2_.refs_4_, bf16[1024,1024]{1,0:T(8,128)(2,1)} %get-tuple-element.136.refs_2_, ...), custom_call_target="tpu_custom_call" | custom-call | flops 99999997952 | bytes 335544320 | tf_op jit(solution)/shard_map/feed_out/pallas_call | solution.py:61
  462.7 14.5 %tokens_back.1 = (f32[1024,1024]{1,0:T(8,128)}, f32[8,1024]{1,0:T(8,128)}) custom-call(bf16[1024,512]{1,0:T(8,128)(2,1)} %get-tuple-element.165.refs_5_.refs_7_.refs_0_, bf16[1024,1024]{1,0:T(8,128)(2,1)} %get-tuple-element.166.refs_6_.refs_1_, bf16[1024,1024]{1,0:T(8,128)(2,1)} %get-tuple-element.157.refs_2_.refs_10_, bf16[1024,1024]{1,0:T(8,128)(2,1)} %refs_3_.10, ...), custom_call_target="tpu_custom_call" | custom-call | flops 140000002048 | bytes 503316480 | tf_op jit(solution)/shard_map/tokens_back/pallas_call | solution.py:61
  477.2 10.0 %collective-permute-done.40.refs_2_.refs_4_ = bf16[256,3072]{1,0:T(8,128)(2,1)} collective-permute-done((bf16[256,3072]{1,0:T(8,128)(2,1)}, bf16[256,3072]{1,0:T(8,128)(2,1)}, u32[]{:S(2)}, u32[]{:S(2)}) %collective-permute-start.40) | collective-permute-done | bytes 1572896 | tf_op jit(solution)/shard_map/ppermute | solution.py:1023
  487.2 4.0 sort_rows.3
  491.2 9.0 %all-reduce.2.cloned.1.call-done.refs_2_ = bf16[128,3712]{1,0:T(8,128)(2,1)} async-done(((bf16[128,3712]{1,0:T(8,128)(2,1)}), bf16[128,3712]{1,0:T(8,128)(2,1)}) %all-reduce.2.cloned.1.call-update) | async-done | bytes 950288 | tf_op jit(solution)/shard_map/psum | solution.py:1201
  503.3 4.5 settle_down.1.refs_8_
  508.7 8.5 %spread.1 = (f32[256,4096]{1,0:T(8,128)}, f32[256,4096]{1,0:T(8,128)}, f32[256]{0:T(256)}) custom-call(s32[49]{0:T(128)} %stack.149.refs_0_, f32[256,1]{1,0:T(8,128)} %copy.33.refs_1_, bf16[256,4096]{1,0:T(8,128)(2,1)} %refs_2_.5, bf16[256,4096]{1,0:T(8,128)(2,1)} %refs_3_.11, bf16[256,2048]{1,0:T(8,128)(2,1)} %get-tuple-element.171.refs_5_.refs_4_, ...), custom_call_target="tpu_custom_call" | custom-call | flops 20000000 | bytes 335544320 | tf_op jit(solution)/shard_map/spread/pallas_call | solution.py:61
  517.3 6.2 %collective-permute-done.38.refs_3_ = bf16[128,3712]{1,0:T(8,128)(2,1)S(1)} collective-permute-done((bf16[128,3712]{1,0:T(8,128)(2,1)}, bf16[128,3712]{1,0:T(8,128)(2,1)S(1)}, u32[]{:S(2)}, u32[]{:S(2)}) %collective-permute-start.38) | collective-permute-done | bytes 950304 | tf_op jit(solution)/shard_map/ppermute | solution.py:1023
  524.3 4.9 settle_mixer.1
  (169 shorter events, 69.2 us)
Async XLA Ops:
  7.2 276.5 %reduce-scatter.3.cloned.1.call-start = ((), (), s32[]{:S(2)}) async-start(), calls=%async_computation.2 | async-start | bytes 1966080 | tf_op jit(solution)/shard_map/reduce_scatter | solution.py:1124
  11.7 14.0 %collective-permute-start.1 = (bf16[64,3712]{1,0:T(8,128)(2,1)}, bf16[64,3712]{1,0:T(8,128)(2,1)S(1)}, u32[]{:S(2)}, u32[]{:S(2)}) collective-permute-start(bf16[64,3712]{1,0:T(8,128)(2,1)} %get-tuple-element.105), channel_id=1, source_target_pairs={{0,2},{2,0},{1,3},{3,1},{4,6},{6,4},{5,7},{7,5},{8,10},{10,8},{9,1... | collective-permute-start | bytes 1425416 | tf_op jit(solution)/shard_map/ppermute | solution.py:1023
  25.8 30.3 %collective-permute-start.9 = (bf16[1024,1024]{1,0:T(8,128)(2,1)S(1)}, bf16[1024,1024]{1,0:T(8,128)(2,1)}, u32[]{:S(2)}, u32[]{:S(2)}) collective-permute-start(bf16[1024,1024]{1,0:T(8,128)(2,1)S(1)} %copy-done.10), channel_id=1, source_target_pairs={{0,1},{1,0},{2,3},{3,2},{4,5},{5,4},{6,7},{7,6},{8,9},{9,8},{10,11... | collective-permute-start | bytes 6291464 | tf_op jit(solution)/shard_map/ppermute | solution.py:1023
  25.8 29.6 %collective-permute-start = (bf16[256,3712]{1,0:T(8,128)(2,1)}, bf16[256,3712]{1,0:T(8,128)(2,1)}, u32[]{:S(2)}, u32[]{:S(2)}) collective-permute-start(bf16[256,3712]{1,0:T(8,128)(2,1)} %get-tuple-element.104.refs_4_.refs_2_), channel_id=1, source_target_pairs={{0,1},{1,0},{2,3},{3,2},{4,5},{5,4},{6,7},{7,6},{8,9},{9,8},{10,11... | collective-permute-start | bytes 5701640 | tf_op jit(solution)/shard_map/ppermute | solution.py:1023
  26.3 12.8 %collective-permute-start.2 = (bf16[64,3712]{1,0:T(8,128)(2,1)S(1)}, bf16[64,3712]{1,0:T(8,128)(2,1)S(1)}, u32[]{:S(2)}, u32[]{:S(2)}) collective-permute-start(bf16[64,3712]{1,0:T(8,128)(2,1)S(1)} %collective-permute-done.1.refs_4_), channel_id=1, source_target_pairs={{0,4},{4,0},{1,5},{5,1},{2,6},{6,2},{3,7},{7,3},{8,12},{12,8},{9,1... | collective-permute-start | bytes 1425416 | tf_op jit(solution)/shard_map/ppermute | solution.py:1023
  28.0 12.9 %collective-permute-start.3 = (bf16[64,3712]{1,0:T(8,128)(2,1)S(1)}, bf16[64,3712]{1,0:T(8,128)(2,1)S(1)}, u32[]{:S(2)}, u32[]{:S(2)}) collective-permute-start(bf16[64,3712]{1,0:T(8,128)(2,1)S(1)} %collective-permute-done.1.refs_4_), channel_id=1, source_target_pairs={{0,8},{8,0},{16,24},{24,16},{1,9},{9,1},{17,25},{25,17},{2,10},{10... | collective-permute-start | bytes 1425416 | tf_op jit(solution)/shard_map/ppermute | solution.py:1092
  29.6 11.6 %collective-permute-start.5 = (bf16[64,3712]{1,0:T(8,128)(2,1)S(1)}, bf16[64,3712]{1,0:T(8,128)(2,1)S(1)}, u32[]{:S(2)}, u32[]{:S(2)}) collective-permute-start(bf16[64,3712]{1,0:T(8,128)(2,1)S(1)} %collective-permute-done.1.refs_4_), channel_id=1, source_target_pairs={{0,1},{1,0},{2,3},{3,2},{4,5},{5,4},{6,7},{7,6},{8,9},{9,8},{10,11... | collective-permute-start | bytes 1425416 | tf_op jit(solution)/shard_map/ppermute | solution.py:1023
  39.1 31.0 %collective-permute-start.13 = (bf16[256,2048]{1,0:T(8,128)(2,1)}, bf16[256,2048]{1,0:T(8,128)(2,1)}, u32[]{:S(2)}, u32[]{:S(2)}) collective-permute-start(bf16[256,2048]{1,0:T(8,128)(2,1)} %get-tuple-element.122), channel_id=1, source_target_pairs={{0,2},{1,3},{2,0},{3,1},{4,7},{5,6},{6,5},{7,4},{8,10},{9,11},{10,... | collective-permute-start | bytes 3145736 | tf_op jit(solution)/shard_map/ppermute | solution.py:1104
  40.9 12.6 %collective-permute-start.4 = (bf16[64,3712]{1,0:T(8,128)(2,1)S(1)}, bf16[64,3712]{1,0:T(8,128)(2,1)S(1)}, u32[]{:S(2)}, u32[]{:S(2)}) collective-permute-start(bf16[64,3712]{1,0:T(8,128)(2,1)S(1)} %collective-permute-done.3.refs_6_), channel_id=1, source_target_pairs={{0,4},{4,0},{1,5},{5,1},{2,6},{6,2},{3,7},{7,3},{8,12},{12,8},{9,1... | collective-permute-start | bytes 1425416 | tf_op jit(solution)/shard_map/ppermute | solution.py:1023
  41.2 12.3 %collective-permute-start.6 = (bf16[64,3712]{1,0:T(8,128)(2,1)S(1)}, bf16[64,3712]{1,0:T(8,128)(2,1)S(1)}, u32[]{:S(2)}, u32[]{:S(2)}) collective-permute-start(bf16[64,3712]{1,0:T(8,128)(2,1)S(1)} %collective-permute-done.2.refs_5_), channel_id=1, source_target_pairs={{0,1},{1,0},{2,3},{3,2},{4,5},{5,4},{6,7},{7,6},{8,9},{9,8},{10,11... | collective-permute-start | bytes 1425416 | tf_op jit(solution)/shard_map/ppermute | solution.py:1023
  53.5 1.8 collective-permute-start.7
  53.5 2.5 collective-permute-start.8
  69.6 26.3 %collective-permute-start.10 = (bf16[512,1024]{1,0:T(8,128)(2,1)}, bf16[512,1024]{1,0:T(8,128)(2,1)S(1)}, u32[]{:S(2)}, u32[]{:S(2)}) collective-permute-start(bf16[512,1024]{1,0:T(8,128)(2,1)} %get-tuple-element.117), channel_id=1, source_target_pairs={{0,2},{2,0},{1,3},{3,1},{4,6},{6,4},{5,7},{7,5},{8,10},{10,8},{9,1... | collective-permute-start | bytes 3145736 | tf_op jit(solution)/shard_map/ppermute | solution.py:1023
  70.1 34.5 %collective-permute-start.14 = (bf16[256,2048]{1,0:T(8,128)(2,1)}, bf16[256,2048]{1,0:T(8,128)(2,1)S(1)}, u32[]{:S(2)}, u32[]{:S(2)}) collective-permute-start(bf16[256,2048]{1,0:T(8,128)(2,1)} %collective-permute-done.13.refs_7_), channel_id=1, source_target_pairs={{0,4},{4,0},{1,5},{5,1},{2,6},{6,2},{3,7},{7,3},{8,12},{12,8},{9,1... | collective-permute-start | bytes 3145736 | tf_op jit(solution)/shard_map/ppermute | solution.py:1023
  72.9 34.0 %collective-permute-start.12 = (bf16[512,2048]{1,0:T(8,128)(2,1)}, bf16[512,2048]{1,0:T(8,128)(2,1)}, u32[]{:S(2)}, u32[]{:S(2)}) collective-permute-start(bf16[512,2048]{1,0:T(8,128)(2,1)} %get-tuple-element.120), channel_id=1, source_target_pairs={{0,1},{1,0},{2,3},{3,2},{4,5},{5,4},{6,7},{7,6},{8,9},{9,8},{10,11... | collective-permute-start | bytes 6291464 | tf_op jit(solution)/shard_map/ppermute | solution.py:1023
  72.9 57.2 %collective-permute-start.15 = (bf16[256,2048]{1,0:T(8,128)(2,1)}, bf16[256,2048]{1,0:T(8,128)(2,1)}, u32[]{:S(2)}, u32[]{:S(2)}) collective-permute-start(bf16[256,2048]{1,0:T(8,128)(2,1)} %get-tuple-element.128), channel_id=1, source_target_pairs={{0,2},{1,3},{2,0},{3,1},{4,7},{5,6},{6,5},{7,4},{8,10},{9,11},{10,... | collective-permute-start | bytes 3145736 | tf_op jit(solution)/shard_map/ppermute | solution.py:1104
  104.1 4.5 collective-permute-start.11
  104.1 61.0 %collective-permute-start.17 = (bf16[512,1024]{1,0:T(8,128)(2,1)}, bf16[512,1024]{1,0:T(8,128)(2,1)}, u32[]{:S(2)}, u32[]{:S(2)}) collective-permute-start(bf16[512,1024]{1,0:T(8,128)(2,1)} %get-tuple-element.131), channel_id=1, source_target_pairs={{0,2},{2,0},{1,3},{3,1},{4,6},{6,4},{5,7},{7,5},{8,10},{10,8},{9,1... | collective-permute-start | bytes 3145736 | tf_op jit(solution)/shard_map/ppermute | solution.py:1023
  130.1 35.0 %collective-permute-start.16 = (bf16[256,2048]{1,0:T(8,128)(2,1)}, bf16[256,2048]{1,0:T(8,128)(2,1)}, u32[]{:S(2)}, u32[]{:S(2)}) collective-permute-start(bf16[256,2048]{1,0:T(8,128)(2,1)} %collective-permute-done.15.refs_7_), channel_id=1, source_target_pairs={{0,4},{4,0},{1,5},{5,1},{2,6},{6,2},{3,7},{7,3},{8,12},{12,8},{9,1... | collective-permute-start | bytes 3145736 | tf_op jit(solution)/shard_map/ppermute | solution.py:1023
  140.5 46.0 %collective-permute-start.19 = (bf16[512,1024]{1,0:T(8,128)(2,1)}, bf16[512,1024]{1,0:T(8,128)(2,1)}, u32[]{:S(2)}, u32[]{:S(2)}) collective-permute-start(bf16[512,1024]{1,0:T(8,128)(2,1)} %get-tuple-element.133.refs_10_), channel_id=1, source_target_pairs={{0,4},{4,0},{1,5},{5,1},{2,6},{6,2},{3,7},{7,3},{8,12},{12,8},{9,1... | collective-permute-start | bytes 3145736 | tf_op jit(solution)/shard_map/ppermute | solution.py:1023
  164.6 26.2 %collective-permute-start.18 = (bf16[256,2048]{1,0:T(8,128)(2,1)}, bf16[256,2048]{1,0:T(8,128)(2,1)}, u32[]{:S(2)}, u32[]{:S(2)}) collective-permute-start(bf16[256,2048]{1,0:T(8,128)(2,1)} %get-tuple-element.134.refs_11_), channel_id=1, source_target_pairs={{0,2},{2,0},{1,3},{3,1},{4,6},{6,4},{5,7},{7,5},{8,10},{10,8},{9,1... | collective-permute-start | bytes 3145736 | tf_op jit(solution)/shard_map/ppermute | solution.py:1023
  189.3 45.9 %collective-permute-start.21 = (bf16[256,1024]{1,0:T(8,128)(2,1)}, bf16[256,1024]{1,0:T(8,128)(2,1)}, u32[]{:S(2)}, u32[]{:S(2)}) collective-permute-start(bf16[256,1024]{1,0:T(8,128)(2,1)} %top_sum.4.refs_3_), channel_id=1, source_target_pairs={{0,2},{2,0},{1,3},{3,1},{4,6},{6,4},{5,7},{7,5},{8,10},{10,8},{9,1... | collective-permute-start | bytes 1572872 | tf_op jit(solution)/shard_map/ppermute | solution.py:1023
  194.2 42.4 %collective-permute-start.23 = (bf16[256,2048]{1,0:T(8,128)(2,1)}, bf16[256,2048]{1,0:T(8,128)(2,1)}, u32[]{:S(2)}, u32[]{:S(2)}) collective-permute-start(bf16[256,2048]{1,0:T(8,128)(2,1)} %top_sum.5.refs_4_), channel_id=1, source_target_pairs={{0,4},{4,0},{1,5},{5,1},{2,6},{6,2},{3,7},{7,3},{8,12},{12,8},{9,1... | collective-permute-start | bytes 3145736 | tf_op jit(solution)/shard_map/ppermute | solution.py:1023
  210.0 33.3 %collective-permute-start.20 = (bf16[1024,1024]{1,0:T(8,128)(2,1)}, bf16[1024,1024]{1,0:T(8,128)(2,1)}, u32[]{:S(2)}, u32[]{:S(2)}) collective-permute-start(bf16[1024,1024]{1,0:T(8,128)(2,1)} %feed_back_partner.1.refs_7_), channel_id=1, source_target_pairs={{0,1},{1,0},{2,3},{3,2},{4,5},{5,4},{6,7},{7,6},{8,9},{9,8},{10,11... | collective-permute-start | bytes 6291464 | tf_op jit(solution)/shard_map/ppermute | solution.py:1023
  210.0 26.7 %collective-permute-start.22 = (bf16[256,2048]{1,0:T(8,128)(2,1)}, bf16[256,2048]{1,0:T(8,128)(2,1)}, u32[]{:S(2)}, u32[]{:S(2)}) collective-permute-start(bf16[256,2048]{1,0:T(8,128)(2,1)} %get-tuple-element.144), channel_id=1, source_target_pairs={{0,2},{2,0},{1,3},{3,1},{4,6},{6,4},{5,7},{7,5},{8,10},{10,8},{9,1... | collective-permute-start | bytes 3145736 | tf_op jit(solution)/shard_map/ppermute | solution.py:1023
  220.0 43.7 %collective-permute-start.25 = (bf16[512,1024]{1,0:T(8,128)(2,1)}, bf16[512,1024]{1,0:T(8,128)(2,1)}, u32[]{:S(2)}, u32[]{:S(2)}) collective-permute-start(bf16[512,1024]{1,0:T(8,128)(2,1)} %get-tuple-element.145.refs_10_), channel_id=1, source_target_pairs={{0,4},{4,0},{1,5},{5,1},{2,6},{6,2},{3,7},{7,3},{8,12},{12,8},{9,1... | collective-permute-start | bytes 3145736 | tf_op jit(solution)/shard_map/ppermute | solution.py:1023
  235.2 32.8 %collective-permute-start.24 = (bf16[256,2048]{1,0:T(8,128)(2,1)}, bf16[256,2048]{1,0:T(8,128)(2,1)}, u32[]{:S(2)}, u32[]{:S(2)}) collective-permute-start(bf16[256,2048]{1,0:T(8,128)(2,1)} %get-tuple-element.146.refs_7_), channel_id=1, source_target_pairs={{0,2},{2,0},{1,3},{3,1},{4,6},{6,4},{5,7},{7,5},{8,10},{10,8},{9,1... | collective-permute-start | bytes 3145736 | tf_op jit(solution)/shard_map/ppermute | solution.py:1023
  242.7 91.8 %all-gather.3.cloned.1.call-start = ((), (), s32[]{:S(2)}) async-start(), calls=%async_computation.3 | async-start | bytes 1966080 | tf_op jit(solution)/shard_map/all_gather | solution.py:1127
  242.8 54.7 %collective-permute-start.27 = (bf16[256,2048]{1,0:T(8,128)(2,1)}, bf16[256,2048]{1,0:T(8,128)(2,1)}, u32[]{:S(2)}, u32[]{:S(2)}) collective-permute-start(bf16[256,2048]{1,0:T(8,128)(2,1)} %get-tuple-element.155), channel_id=1, source_target_pairs={{0,2},{2,0},{1,3},{3,1},{4,6},{6,4},{5,7},{7,5},{8,10},{10,8},{9,1... | collective-permute-start | bytes 3145736 | tf_op jit(solution)/shard_map/ppermute | solution.py:1023
  266.5 31.0 %collective-permute-start.26 = (bf16[256,1024]{1,0:T(8,128)(2,1)}, bf16[256,1024]{1,0:T(8,128)(2,1)}, u32[]{:S(2)}, u32[]{:S(2)}) collective-permute-start(bf16[256,1024]{1,0:T(8,128)(2,1)} %top_sum.6.refs_3_), channel_id=1, source_target_pairs={{0,2},{2,0},{1,3},{3,1},{4,6},{6,4},{5,7},{7,5},{8,10},{10,8},{9,1... | collective-permute-start | bytes 1572872 | tf_op jit(solution)/shard_map/ppermute | solution.py:1023
  271.4 26.1 %collective-permute-start.28 = (bf16[256,2048]{1,0:T(8,128)(2,1)}, bf16[256,2048]{1,0:T(8,128)(2,1)}, u32[]{:S(2)}, u32[]{:S(2)}) collective-permute-start(bf16[256,2048]{1,0:T(8,128)(2,1)} %top_sum.7.refs_5_), channel_id=1, source_target_pairs={{0,4},{4,0},{1,5},{5,1},{2,6},{6,2},{3,7},{7,3},{8,12},{12,8},{9,1... | collective-permute-start | bytes 3145736 | tf_op jit(solution)/shard_map/ppermute | solution.py:1023
  283.6 52.1 %collective-permute-start.30 = (bf16[1024,128]{1,0:T(8,128)(2,1)}, bf16[1024,128]{1,0:T(8,128)(2,1)}, u32[]{:S(2)}, u32[]{:S(2)}) collective-permute-start(bf16[1024,128]{1,0:T(8,128)(2,1)} %get-tuple-element.162.refs_3_.refs_7_), channel_id=1, source_target_pairs={{0,1},{1,0},{2,3},{3,2},{4,5},{5,4},{6,7},{7,6},{8,9},{9,8},{10,11... | collective-permute-start | bytes 786440 | tf_op jit(solution)/shard_map/ppermute | solution.py:1023
  296.9 38.9 %collective-permute-start.29 = (bf16[512,2048]{1,0:T(8,128)(2,1)}, bf16[512,2048]{1,0:T(8,128)(2,1)}, u32[]{:S(2)}, u32[]{:S(2)}) collective-permute-start(bf16[512,2048]{1,0:T(8,128)(2,1)} %get-tuple-element.158.refs_7_), channel_id=1, source_target_pairs={{0,1},{1,0},{2,3},{3,2},{4,5},{5,4},{6,7},{7,6},{8,9},{9,8},{10,11... | collective-permute-start | bytes 6291464 | tf_op jit(solution)/shard_map/ppermute | solution.py:1023
  297.4 109.8 %reduce-scatter.5.cloned.1.call-start = ((), (), s32[]{:S(2)}) async-start(), calls=%async_computation.4 | async-start | bytes 1966080 | tf_op jit(solution)/shard_map/reduce_scatter | solution.py:1124
  303.5 140.2 %all-gather.5.cloned.1.call-start = ((), (), s32[]{:S(2)}) async-start(), calls=%async_computation.5 | async-start | bytes 1966080 | tf_op jit(solution)/shard_map/all_gather | solution.py:1127
  340.3 63.5 %collective-permute-start.32 = (bf16[256,2176]{1,0:T(8,128)(2,1)}, bf16[256,2176]{1,0:T(8,128)(2,1)}, u32[]{:S(2)}, u32[]{:S(2)}) collective-permute-start(bf16[256,2176]{1,0:T(8,128)(2,1)} %get-tuple-element.164.refs_11_), channel_id=1, source_target_pairs={{0,2},{2,0},{1,3},{3,1},{4,6},{6,4},{5,7},{7,5},{8,10},{10,8},{9,1... | collective-permute-start | bytes 3342344 | tf_op jit(solution)/shard_map/ppermute | solution.py:1023
  362.7 36.0 %collective-permute-start.33 = (bf16[256,3072]{1,0:T(8,128)(2,1)S(1)}, bf16[256,3072]{1,0:T(8,128)(2,1)S(1)}, u32[]{:S(2)}, u32[]{:S(2)}) collective-permute-start(bf16[256,3072]{1,0:T(8,128)(2,1)S(1)} %copy-done.15), channel_id=1, source_target_pairs={{0,4},{4,0},{1,5},{5,1},{2,6},{6,2},{3,7},{7,3},{8,12},{12,8},{9,1... | collective-permute-start | bytes 4718600 | tf_op jit(solution)/shard_map/ppermute | solution.py:1023
  374.1 34.4 %collective-permute-start.31 = (bf16[512,1536]{1,0:T(8,128)(2,1)}, bf16[512,1536]{1,0:T(8,128)(2,1)}, u32[]{:S(2)}, u32[]{:S(2)}) collective-permute-start(bf16[512,1536]{1,0:T(8,128)(2,1)} %get-tuple-element.168.refs_3_), channel_id=1, source_target_pairs={{0,1},{1,0},{2,3},{3,2},{4,5},{5,4},{6,7},{7,6},{8,9},{9,8},{10,11... | collective-permute-start | bytes 4718600 | tf_op jit(solution)/shard_map/ppermute | solution.py:1023
  412.3 18.4 %collective-permute-start.35 = (bf16[256,1536]{1,0:T(8,128)(2,1)}, bf16[256,1536]{1,0:T(8,128)(2,1)S(1)}, u32[]{:S(2)}, u32[]{:S(2)}) collective-permute-start(bf16[256,1536]{1,0:T(8,128)(2,1)} %get-tuple-element.173.refs_4_), channel_id=1, source_target_pairs={{0,2},{2,0},{1,3},{3,1},{4,6},{6,4},{5,7},{7,5},{8,10},{10,8},{9,1... | collective-permute-start | bytes 2359304 | tf_op jit(solution)/shard_map/ppermute | solution.py:1023
  412.8 32.2 %collective-permute-start.34 = (bf16[128,2176]{1,0:T(8,128)(2,1)}, bf16[128,2176]{1,0:T(8,128)(2,1)}, u32[]{:S(2)}, u32[]{:S(2)}) collective-permute-start(bf16[128,2176]{1,0:T(8,128)(2,1)} %get-tuple-element.174), channel_id=1, source_target_pairs={{0,4},{4,0},{1,5},{5,1},{2,6},{6,2},{3,7},{7,3},{8,12},{12,8},{9,1... | collective-permute-start | bytes 1671176 | tf_op jit(solution)/shard_map/ppermute | solution.py:1023
  414.3 93.5 %collective-permute-start.39 = (bf16[256,2048]{1,0:T(8,128)(2,1)}, bf16[256,2048]{1,0:T(8,128)(2,1)}, u32[]{:S(2)}, u32[]{:S(2)}) collective-permute-start(bf16[256,2048]{1,0:T(8,128)(2,1)} %get-tuple-element.181), channel_id=1, source_target_pairs={{0,1},{1,0},{2,3},{3,2},{4,5},{5,4},{6,7},{7,6},{8,9},{9,8},{10,11... | collective-permute-start | bytes 3145736 | tf_op jit(solution)/shard_map/ppermute | solution.py:1023
  434.6 10.4 %collective-permute-start.36 = (bf16[128,1536]{1,0:T(8,128)(2,1)}, bf16[128,1536]{1,0:T(8,128)(2,1)}, u32[]{:S(2)}, u32[]{:S(2)}) collective-permute-start(bf16[128,1536]{1,0:T(8,128)(2,1)} %get-tuple-element.177), channel_id=1, source_target_pairs={{0,4},{4,0},{1,5},{5,1},{2,6},{6,2},{3,7},{7,3},{8,12},{12,8},{9,1... | collective-permute-start | bytes 1179656 | tf_op jit(solution)/shard_map/ppermute | solution.py:1023
  448.2 4.5 collective-permute-start.37
  449.5 50.7 %all-reduce.2.cloned.1.call-start = ((), (), s32[]{:S(2)}) async-start(), calls=%async_computation.6 | async-start | bytes 1900544 | tf_op jit(solution)/shard_map/psum | solution.py:1201
  450.0 37.2 %collective-permute-start.40 = (bf16[256,3072]{1,0:T(8,128)(2,1)}, bf16[256,3072]{1,0:T(8,128)(2,1)}, u32[]{:S(2)}, u32[]{:S(2)}) collective-permute-start(bf16[256,3072]{1,0:T(8,128)(2,1)} %all-gather.5.cloned.1.call-done.refs_1_.refs_3_), channel_id=1, source_target_pairs={{0,4},{4,0},{1,5},{5,1},{2,6},{6,2},{3,7},{7,3},{8,12},{12,8},{9,1... | collective-permute-start | bytes 4718600 | tf_op jit(solution)/shard_map/ppermute | solution.py:1023
  477.2 24.5 %copy-start.31 = (bf16[256]{0:T(256)(128)(2,1)S(1)}, bf16[256]{0:T(256)(128)(2,1)}, u32[]{:S(2)}) copy-start(bf16[256]{0:T(256)(128)(2,1)} %refs_2_.3) | copy-start | bytes 1540
  491.2 16.5 %collective-permute-start.41 = (bf16[256,2048]{1,0:T(8,128)(2,1)}, bf16[256,2048]{1,0:T(8,128)(2,1)S(1)}, u32[]{:S(2)}, u32[]{:S(2)}) collective-permute-start(bf16[256,2048]{1,0:T(8,128)(2,1)} %get-tuple-element.184), channel_id=1, source_target_pairs={{0,1},{1,0},{2,3},{3,2},{4,5},{5,4},{6,7},{7,6},{8,9},{9,8},{10,11... | collective-permute-start | bytes 3145736 | tf_op jit(solution)/shard_map/ppermute | solution.py:1023
  500.2 23.2 %collective-permute-start.38 = (bf16[128,3712]{1,0:T(8,128)(2,1)}, bf16[128,3712]{1,0:T(8,128)(2,1)S(1)}, u32[]{:S(2)}, u32[]{:S(2)}) collective-permute-start(bf16[128,3712]{1,0:T(8,128)(2,1)} %all-reduce.2.cloned.1.call-done.refs_2_), channel_id=1, source_target_pairs={{0,4},{4,0},{1,5},{5,1},{2,6},{6,2},{3,7},{7,3},{8,12},{12,8},{9,1... | collective-permute-start | bytes 2850824 | tf_op jit(solution)/shard_map/ppermute | solution.py:1023
  (32 other events, 262.4 us)
Sparse Core Ops, SparseCore 0:
  242.9 35.7 reduce-scatter.2
  297.5 36.9 all-gather.2
  336.8 34.1 reduce-scatter.4
  408.6 35.0 all-gather.4
  452.4 47.7 all-reduce.1
